TPU v7x, 128 devices: a whole 4x4x4 slice. The times are simulated.
128 devices in a mesh: head: 8 (over x, core), expert: 16 (over z, y).
Axes of the slice: x: 4, y: 4, z: 4, core: 2. Of those that a mesh axis runs over, the one named last changes fastest.
Arguments:
- queries: bfloat16 [16, 128, 6144], P('expert', None, 'head')
- key_states: bfloat16 [16, 128, 1024], P('expert', None, 'head')
- corrupted_value_state: bfloat16 [16, 128, 1024], P('expert', None, 'head'), may hold values from -6 to 6
- clean_heads: bfloat16 [16, 128, 6144], P('expert', None, 'head'), may hold values from -6 to 6
- patch_heads: int32 [16, 8], P('expert'), may hold values from 0 to 47, as said below
- out_weight: bfloat16 [6144, 6144], P('head', 'expert'), may hold values from -0.078125 to 0.078125
- residual: bfloat16 [16, 128, 6144], P('expert', 'head'), may hold values from -6 to 6
- norm_gain: float32 [6144], replicated, may hold values from 0.1 to 1.9
- expert_ids: int32 [16, 128, 2], P('expert', 'head'), may hold values from 0 to 7, all different within a row; in each aligned block of 16 rows (0 to 15, 16 to 31, ..., all dimensions but the last counted through in order) at most 6 rows name the same one
- route_weights: float32 [16, 128, 2], P('expert', 'head'), may hold values from 0.1 to 0.9
- gate_weight: bfloat16 [8, 6144, 8192], P('head', None, 'expert'), may hold values from -0.078125 to 0.078125
- up_weight: bfloat16 [8, 6144, 8192], P('head', None, 'expert'), may hold values from -0.078125 to 0.078125
- down_weight: bfloat16 [8, 8192, 6144], P('head', 'expert'), may hold values from -0.0625 to 0.0625
Outputs:
- layer_out: bfloat16 [16, 128, 6144], P('expert', 'head')
Inputs may be any that keep to these rules, and one draw needn't show every extreme that they name: `expert_ids`: each row names 2 different experts; among the rows of one device (aligned blocks of 16 positions of a prompt) no expert is named more than 6 times, and 6 is reached. `patch_heads`: each row names 8 different heads.
All inputs are finite; a program needn't handle non-finite values.
Results may differ from a plain program's by a relative error of at most 0.023.
Values may be sent and summed in bfloat16 or wider, within the bound.
No kernel may reach another device: no remote copies, remote signals or barrier semaphores. Data moves between devices by JAX's collectives and lax.ppermute only.
A program may use at most 128 MiB of HBM per device.

v0:
```python
import math

import jax
import jax.numpy as jnp
from jax import lax
from jax.experimental import pallas as pl
from jax.experimental.pallas import tpu as pltpu
from jax.sharding import PartitionSpec as P

HEAD_SIZE = 128
RING = 4
NEAR_FIRST = (0, -1, 1, 2)
FAR_FIRST = (2, 1, -1, 0)
BF = jnp.bfloat16
F32 = jnp.float32


def ring_pairs(near, step):
    pairs = []
    for head in range(8):
        for z in range(RING):
            for y in range(RING):
                if near == (head % 2 == 0):
                    target = ((z + step) % RING) * RING + y
                else:
                    target = z * RING + (y + step) % RING
                pairs.append((head * 16 + z * RING + y, head * 16 + target))
    return pairs


def send(block, near, step):
    return lax.ppermute(block, ("head", "expert"), ring_pairs(near, step))


def gather_pieces(block, direct=False, after=None):
    half = block.shape[0] // 2
    up = send(block, True, 1)
    down = send(block, True, -1)
    first = jnp.stack([block, up])
    if direct:
        far = send(block, True, 2)
    else:
        far_low = send(up[:half], True, 1)
        far_high = send(down[half:], True, -1)
        if after is not None:
            far_low, far_high, after = lax.optimization_barrier((far_low, far_high, after))
        far = jnp.concatenate([far_low, far_high], axis=0)
    first_up = send(first, False, 1)
    first_down = send(first, False, -1)
    second = jnp.stack([down, far])
    second_up = send(second, False, 1)
    second_down = send(second, False, -1)
    return (first, second, first_up, first_down, second_up, second_down), after


def forward(first_up, second_down):
    return send(first_up, False, 1), send(second_down, False, -1)


PIECE_NEAR = ((0, -1), (1, 2), (0, -1), (0, -1), (1, 2), (1, 2), (0, -1), (1, 2))
PIECE_FAR = (0, 0, -1, 1, -1, 1, 2, 2)


def in_hbm(array):
    return pltpu.with_memory_space_constraint(array, pltpu.HBM)


def project_kernel(place, *refs):
    blocks, (weight, resid, gain, targets, projected, slots, total, rows) = refs[:8], refs[8:]
    count, width = projected.shape[0], projected.shape[2]
    acc = None
    for group in range(weight.shape[0]):
        block = jnp.concatenate([ref[:, group] for ref in blocks], axis=0)
        block = block.reshape(-1, block.shape[-1])
        term = jnp.dot(block, weight[group], preferred_element_type=F32)
        acc = term if acc is None else acc + term
    total[...] = acc.reshape(total.shape)
    for prompt in range(count):
        value = total[place[prompt]]
        projected[prompt] = value.astype(BF)
        hidden = value + resid[prompt][:, :width].astype(F32)
        rows[prompt] = (hidden * gain[...]).astype(BF)
    tokens = rows[...].reshape(-1, width)
    slot_ids = lax.broadcasted_iota(jnp.int32, (slots.shape[0], tokens.shape[0]), 0)
    chosen = (slot_ids == targets[0:1, :]) | (slot_ids == targets[1:2, :])
    dispatch = jnp.where(chosen, 1.0, 0.0).astype(BF)
    slots[...] = jnp.dot(dispatch, tokens, preferred_element_type=F32).astype(BF)


def project(place, blocks, weight, resid, gain, targets, slot_count):
    count, rows = resid.shape[0], resid.shape[1]
    width = weight.shape[2]
    whole = pl.BlockSpec(memory_space=pltpu.VMEM)
    return pl.pallas_call(
        project_kernel,
        out_shape=[
            jax.ShapeDtypeStruct((count, rows, width), BF),
            jax.ShapeDtypeStruct((slot_count, width), BF),
        ],
        in_specs=[pl.BlockSpec(memory_space=pltpu.SMEM)] + [whole] * (len(blocks) + 4),
        out_specs=[whole, whole],
        scratch_shapes=[
            pltpu.VMEM((count, rows, width), F32),
            pltpu.VMEM((count, rows, width), BF),
        ],
        compiler_params=pltpu.CompilerParams(vmem_limit_bytes=24 * 2**20),
        cost_estimate=pl.CostEstimate(
            flops=2 * count * rows * 6144 * width, bytes_accessed=10 * 2**20, transcendentals=0
        ),
    )(place, *blocks, weight, resid, gain, targets)


DOWN_STEP = 768


def down_scratch(rows, depth, wide, parts):
    chunks = wide // DOWN_STEP
    return [
        pltpu.VMEM((chunks, depth, DOWN_STEP), BF),
        pltpu.VMEM((chunks, rows, DOWN_STEP), BF),
        pltpu.SemaphoreType.DMA((chunks,)),
        pltpu.SemaphoreType.DMA((chunks, parts)),
    ]


def down_reads(weight, held, sems, start):
    return [
        pltpu.make_async_copy(
            weight.at[:, pl.ds(start + chunk * DOWN_STEP, DOWN_STEP)],
            held.at[chunk],
            sems.at[chunk],
        )
        for chunk in range(held.shape[0])
    ]


def down_products(left, copies, held, made, out_sems, outs):
    leaving = []
    for chunk, copy in enumerate(copies):
        copy.wait()
        made[chunk] = jnp.dot(left, held[chunk], preferred_element_type=F32).astype(BF)
        at = 0
        for index, out in enumerate(outs):
            leaving.append(
                pltpu.make_async_copy(
                    made.at[chunk, pl.ds(at, out.shape[0])],
                    out.at[:, pl.ds(chunk * DOWN_STEP, DOWN_STEP)],
                    out_sems.at[chunk, index],
                )
            )
            leaving[-1].start()
            at += out.shape[0]
    for copy in leaving:
        copy.wait()


def gate_up_kernel(steps, finish, begun, parts, order, *refs):
    count = sum(len(shapes) for shapes, _ in steps)
    blocks, refs = refs[:count], refs[count:]
    gate, up, inverse_gain = refs[:3]
    refs = refs[3:]
    before, refs = (refs[:3], refs[3:]) if begun else ((), refs)
    if finish:
        row_of, down_weight, out = refs[:3]
        parts, refs = refs[3 : 3 + parts], refs[3 + parts :]
        gate_sum, up_sum, square_sum, down_held, down_made, down_in, down_out = refs[:7]
        refs = refs[7:]
    else:
        sums_out, refs = refs[:3], refs[3:]
        gate_sum, up_sum, square_sum = refs[:3]
        refs = refs[3:]
    held, weights, sems = refs[:count], refs[count : count + 2 * len(steps)], refs[-1]
    carried = refs[count + 2 * len(steps) : -1]

    copies, at, place, sem = [], 0, 0, 0
    for step, (shapes, column) in enumerate(steps):
        mine = []
        for shape in shapes:
            mine.append(pltpu.make_async_copy(blocks[at], held[at], sems.at[sem]))
            at, sem = at + 1, sem + 1
        width = shapes[0][2]
        for index in range(sum(shape[0] for shape in shapes)):
            for source, target in ((gate, weights[2 * step]), (up, weights[2 * step + 1])):
                mine.append(
                    pltpu.make_async_copy(
                        source.at[order[place], pl.ds(column, width)],
                        target.at[pl.ds(index * width, width)],
                        sems.at[sem],
                    )
                )
                sem += 1
            place += 1
        copies.append(mine)
    last = []
    for source, target in zip(before, carried):
        last.append(pltpu.make_async_copy(source, target, sems.at[sem]))
        sem += 1
    down_copies = down_reads(down_weight, down_held, down_in, 0) if finish else []
    for mine in [*copies, last, down_copies]:
        for copy in mine:
            copy.start()
    total = jnp.zeros(square_sum.shape, F32)
    lanes = square_sum.shape[1]
    at, place = 0, 0
    for step, (shapes, column) in enumerate(steps):
        for copy in copies[step]:
            copy.wait()
        pieces = []
        width = shapes[0][2]
        for shape in shapes:
            for index in range(shape[0]):
                pieces.append(held[at][index])
            at += 1
        block = jnp.concatenate(pieces, axis=1)
        gate_term = jnp.dot(block, weights[2 * step][...], preferred_element_type=F32)
        gate_sum[...] = gate_sum[...] + gate_term if step > 0 else gate_term
        up_term = jnp.dot(block, weights[2 * step + 1][...], preferred_element_type=F32)
        up_sum[...] = up_sum[...] + up_term if step > 0 else up_term
        for piece in pieces:
            inverse = inverse_gain[order[place]][:, column : column + width]
            plain = piece.astype(F32) * inverse
            squares = plain * plain
            for lane in range(0, width, lanes):
                total = total + squares[:, lane : lane + lanes]
            place += 1
    if begun:
        for copy in last:
            copy.wait()
        gate_sum[...] = gate_sum[...] + carried[0][...]
        up_sum[...] = up_sum[...] + carried[1][...]
        total = total + carried[2][...]
    if not finish:
        square_sum[...] = total
        leaving = [
            pltpu.make_async_copy(source, target, sems.at[sem - 3 + index])
            for index, (source, target) in enumerate(
                zip((gate_sum, up_sum, square_sum), sums_out)
            )
        ]
        for copy in leaving:
            copy.start()
        for copy in leaving:
            copy.wait()
    else:
        features = 6144
        mean_square = jnp.sum(total, axis=1, keepdims=True) / features
        factor = lax.rsqrt(mean_square + 1e-05)
        gate_act = gate_sum[...] * factor
        up_act = up_sum[...] * factor
        hidden = (gate_act * jax.nn.sigmoid(gate_act) * up_act).astype(BF)
        rows = hidden.shape[0]
        places = lax.broadcasted_iota(jnp.int32, (rows, rows), 1)
        picks = jnp.where(places == row_of[...], 1.0, 0.0).astype(BF)
        left = jnp.dot(picks, hidden, preferred_element_type=F32).astype(BF)
        out[...] = left
        down_products(left, down_copies, down_held, down_made, down_out, parts)


def gate_up(order, steps, gate, up, inverse_gain, sums=None, row_of=None, product=None):
    blocks = [block for group, _ in steps for block in group]
    rows, hidden = blocks[0].shape[1], gate.shape[2]
    shapes = tuple((tuple(block.shape for block in group), column) for group, column in steps)
    finish, begun = row_of is not None, sums is not None
    any_place = pl.BlockSpec(memory_space=pl.ANY)
    whole = pl.BlockSpec(memory_space=pltpu.VMEM)
    sum_shapes = [(rows, hidden), (rows, hidden), (rows, 128)]
    operands = [order, *blocks, gate, up, inverse_gain]
    specs = [pl.BlockSpec(memory_space=pltpu.SMEM)] + [any_place] * (len(blocks) + 2) + [whole]
    if begun:
        operands += [in_hbm(array) for array in sums]
        specs += [any_place] * 3
    scratch = []
    if finish:
        weight, wide, parts = product
        operands += [row_of, weight]
        specs += [whole, any_place]
        out_shape = [jax.ShapeDtypeStruct((rows, hidden), BF)]
        out_shape += [pltpu.HBM((part, wide), BF) for part in parts]
        out_specs = [whole] + [any_place] * len(parts)
        scratch += [pltpu.VMEM(shape, F32) for shape in sum_shapes]
        scratch += down_scratch(rows, hidden, wide, len(parts))
    else:
        out_shape = [pltpu.HBM(shape, F32) for shape in sum_shapes]
        out_specs = [any_place] * 3
        scratch += [pltpu.VMEM(shape, F32) for shape in sum_shapes]
    scratch += [pltpu.VMEM(block.shape, BF) for block in blocks]
    depth, copies = 0, len(blocks)
    for group, _ in steps:
        places = sum(block.shape[0] for block in group)
        scratch += [pltpu.VMEM((places * group[0].shape[2], hidden), BF)] * 2
        depth += places * group[0].shape[2]
        copies += 2 * places
    if begun:
        scratch += [pltpu.VMEM(shape, F32) for shape in sum_shapes]
        copies += 3
    scratch.append(pltpu.SemaphoreType.DMA((copies,)))
    return pl.pallas_call(
        lambda *refs: gate_up_kernel(shapes, finish, begun, len(product[2]) if product else 0, *refs),
        out_shape=out_shape,
        in_specs=specs,
        out_specs=out_specs,
        scratch_shapes=scratch,
        compiler_params=pltpu.CompilerParams(vmem_limit_bytes=48 * 2**20),
        cost_estimate=pl.CostEstimate(
            flops=4 * rows * depth * hidden,
            bytes_accessed=2 * depth * (rows + 2 * hidden),
            transcendentals=0,
        ),
    )(*operands)


def down_kernel(start, hidden, weight, *refs):
    outs, (held, made, sems, out_sems) = refs[:-4], refs[-4:]
    copies = down_reads(weight, held, sems, start)
    for copy in copies:
        copy.start()
    down_products(hidden[...], copies, held, made, out_sems, outs)


def down(hidden, weight, start, wide, parts):
    rows, depth = hidden.shape
    any_place = pl.BlockSpec(memory_space=pl.ANY)
    return pl.pallas_call(
        lambda *refs: down_kernel(start, *refs),
        out_shape=[pltpu.HBM((part, wide), BF) for part in parts],
        in_specs=[pl.BlockSpec(memory_space=pltpu.VMEM), any_place],
        out_specs=[any_place] * len(parts),
        scratch_shapes=down_scratch(rows, depth, wide, len(parts)),
        compiler_params=pltpu.CompilerParams(vmem_limit_bytes=24 * 2**20),
        cost_estimate=pl.CostEstimate(
            flops=2 * rows * depth * wide, bytes_accessed=8 * 2**20, transcendentals=0
        ),
    )(hidden, weight)


def add(*terms):
    total = terms[0].astype(F32)
    for term in terms[1:]:
        total = total + term.astype(F32)
    return total.astype(BF)


def send_far(low, high):
    return send(low, True, 1), send(high, True, -1)


def far_sum(came, plus, minus, own):
    low_came, high_came = came
    half = low_came.shape[0]
    plus = lax.dynamic_update_slice_in_dim(plus, add(plus[:half], low_came), 0, 0)
    minus = lax.dynamic_update_slice_in_dim(minus, add(minus[half:], high_came), half, 0)
    return add(own, send(plus, True, 1), send(minus, True, -1))


def near_sum(blocks):
    came = [send(blocks[at], False, step) for at, step in enumerate(FAR_FIRST[:3])]
    return add(blocks[3], *came)


def attend_kernel(first_head, patch, *refs):
    sources, out, held, sems = refs[:4], refs[4], refs[5:9], refs[9]
    copies = [
        pltpu.make_async_copy(source, target, sems.at[index])
        for index, (source, target) in enumerate(zip(sources, held))
    ]
    for copy in copies:
        copy.start()
    for copy in copies:
        copy.wait()
    query, key, value, clean = held
    length, width = query.shape
    scale = 1.0 / math.sqrt(HEAD_SIZE)
    places = lax.broadcasted_iota(jnp.int32, (length, length), 0)
    causal = places >= lax.broadcasted_iota(jnp.int32, (length, length), 1)
    cuts = [slice(at, at + HEAD_SIZE) for at in range(0, width, HEAD_SIZE)]
    scores = [
        lax.dot_general(query[:, cut], key[...], (((1,), (1,)), ((), ())), preferred_element_type=F32)
        for cut in cuts
    ]
    scores = [jnp.where(causal, score * scale, -jnp.inf) for score in scores]
    raised = [jnp.exp(score - jnp.max(score, axis=1, keepdims=True)) for score in scores]
    probs = [(row / jnp.sum(row, axis=1, keepdims=True)).astype(BF) for row in raised]
    attended = [jnp.dot(prob, value[...], preferred_element_type=F32).astype(BF) for prob in probs]
    for head, cut in enumerate(cuts):
        chosen = patch[0, 0] == first_head[0] + head
        for index in range(1, patch.shape[1]):
            chosen = chosen | (patch[0, index] == first_head[0] + head)
        out[:, cut] = jnp.where(chosen, clean[:, cut], attended[head])


def attend(queries, key_states, corrupted_value_state, clean_heads, patch_heads):
    arrays = [array[0] for array in (queries, key_states, corrupted_value_state, clean_heads)]
    length, width = arrays[0].shape
    first_head = (lax.axis_index("head") * (width // HEAD_SIZE)).reshape(1)
    small = pl.BlockSpec(memory_space=pltpu.SMEM)
    return pl.pallas_call(
        attend_kernel,
        out_shape=jax.ShapeDtypeStruct((length, width), BF),
        in_specs=[small, small] + [pl.BlockSpec(memory_space=pl.ANY)] * 4,
        out_specs=pl.BlockSpec(memory_space=pltpu.VMEM),
        scratch_shapes=[pltpu.VMEM(array.shape, BF) for array in arrays]
        + [pltpu.SemaphoreType.DMA((4,))],
        compiler_params=pltpu.CompilerParams(vmem_limit_bytes=8 * 2**20),
        cost_estimate=pl.CostEstimate(
            flops=4 * length * length * width, bytes_accessed=2**20, transcendentals=0
        ),
    )(first_head, patch_heads, *(in_hbm(array) for array in arrays))


def per_device(
    queries,
    key_states,
    corrupted_value_state,
    clean_heads,
    patch_heads,
    out_weight,
    residual,
    norm_gain,
    expert_ids,
    route_weights,
    gate_weight,
    up_weight,
    down_weight,
):
    heads, experts = lax.axis_size("head"), lax.axis_size("expert")
    e_index = lax.axis_index("expert")
    z_index, y_index = e_index // RING, e_index % RING
    first_core = lax.axis_index("head") % 2 == 0
    near_index, far_index = (
        jnp.where(first_core, z_index, y_index),
        jnp.where(first_core, y_index, z_index),
    )
    tokens, width = residual.shape[1], residual.shape[2]
    top = expert_ids.shape[2]
    capacity = 3 * tokens * top // (2 * heads)
    columns = width // experts

    def place_of(near, far):
        return jnp.where(first_core, near * RING + far, far * RING + near)

    weight_all = lax.all_gather(out_weight, "head", axis=0)
    merged = attend(queries, key_states, corrupted_value_state, clean_heads, patch_heads)
    merged = merged.reshape(heads, tokens, merged.shape[1])
    merged = lax.all_to_all(merged, "head", split_axis=0, concat_axis=0, tiled=True)
    pieces, _ = gather_pieces(merged, direct=True)
    first_up, weight_all = lax.optimization_barrier((pieces[2], weight_all))
    pieces = (*pieces[:2], first_up, *pieces[3:])
    pieces = (*pieces, *forward(pieces[2], pieces[5]))

    pairs = expert_ids.reshape(-1)
    onehot = (pairs[:, None] == jnp.arange(heads)[None, :]).astype(F32)
    earlier = (jnp.arange(pairs.shape[0])[:, None] > jnp.arange(pairs.shape[0])[None, :]).astype(F32)
    ranks = jnp.sum(onehot * jnp.dot(earlier, onehot), axis=1).astype(jnp.int32)
    ranks = ranks.reshape(tokens, top)

    resid = residual[0]
    resid_blocks = resid.reshape(tokens, experts, columns).transpose(1, 0, 2)
    id_block = jnp.concatenate([expert_ids[0], ranks], axis=1).astype(BF)
    id_block = jnp.pad(id_block, ((0, 0), (0, 128 - 2 * top)))
    payload = jnp.concatenate(
        [resid_blocks, jnp.broadcast_to(id_block[None], (experts, tokens, 128))], axis=2
    )
    payload = lax.all_to_all(payload, "expert", split_axis=0, concat_axis=0, tiled=True)
    marks = payload[:, :, columns : columns + 2 * top].astype(jnp.int32)
    prompts = jnp.arange(experts)
    targets = (marks[..., :top] * experts + prompts[:, None, None]) * capacity + marks[..., top:]
    targets = targets.reshape(-1, top).T

    near_steps = jnp.array(PIECE_NEAR)
    far_steps = jnp.array(PIECE_FAR)[:, None]
    order = place_of((near_index + near_steps) % RING, (far_index + far_steps) % RING).reshape(-1)
    at = jnp.arange(experts)
    place = jnp.sum(jnp.where(order[None, :] == at[:, None], at[None, :], 0), axis=1)

    own_gain = lax.dynamic_slice(norm_gain, (e_index * columns,), (columns,))[None]
    projected, slots = project(
        place, pieces, weight_all, payload, own_gain, targets,
        heads * experts * capacity,
    )
    own_projected = lax.all_to_all(projected, "expert", split_axis=0, concat_axis=0, tiled=True)

    slots = slots.reshape(heads, experts * capacity, columns)
    slots = lax.all_to_all(slots, "head", split_axis=0, concat_axis=0, tiled=True)
    pieces, own_projected = gather_pieces(slots.reshape(-1, columns), after=own_projected)
    first, second, first_up, first_down, second_up, second_down = pieces
    gate = in_hbm(gate_weight[0].reshape(experts, columns, -1))
    up = in_hbm(up_weight[0].reshape(experts, columns, -1))
    inverse_gain = (1.0 / norm_gain).reshape(experts, 1, columns)
    sums = gate_up(
        order[:8], [((block,), 0) for block in (first, second, first_up, first_down)],
        gate, up, inverse_gain,
    )
    second_up, second_down, *sums = lax.optimization_barrier((second_up, second_down, *sums))
    far_first, far_second = forward(first_up, second_down)
    sums = gate_up(
        order[8:12], [((second_up,), 0), ((second_down,), 0)], gate, up, inverse_gain, sums=sums
    )

    steps = jnp.array(FAR_FIRST)
    prompt = place_of(
        (near_index + steps[:, None]) % RING, (far_index + steps[None, :]) % RING
    )[:, :, None, None]
    source = jnp.arange(heads)[None, None, :, None]
    slot = jnp.arange(capacity)[None, None, None, :]
    row_of = ((source * experts + prompt) * capacity + slot).reshape(-1, 1)
    rows = heads * experts * capacity // RING
    parts = (rows // 2, rows // 2, rows, rows, rows)
    weight = in_hbm(down_weight[0])
    wide = width // 2
    hidden, *first_parts = gate_up(
        order[12:], [((far_first,), 0), ((far_second,), 0)], gate, up, inverse_gain, sums=sums,
        row_of=row_of, product=(weight, wide, parts),
    )
    own_slots = expert_ids[0] * capacity + ranks
    first_came = send_far(*first_parts[:2])
    last_parts = down(hidden, weight, wide, width - wide, parts)
    low, high, *first_came = lax.optimization_barrier((*last_parts[:2], *first_came))
    last_came = send_far(low, high)
    total = jnp.concatenate(
        [far_sum(first_came, *first_parts[2:]), far_sum(last_came, *last_parts[2:])], axis=1
    )
    totals = near_sum(total.reshape(RING, -1, width))
    totals = totals.reshape(heads, capacity, width)
    returned = lax.all_to_all(totals, "head", split_axis=0, concat_axis=0, tiled=True)
    returned = returned.reshape(heads * capacity, width)
    own_projected = own_projected.transpose(1, 0, 2).reshape(tokens, width)
    layer_out = residual[0].astype(F32) + own_projected.astype(F32)
    for k in range(top):
        pick = (own_slots[:, k : k + 1] == jnp.arange(heads * capacity)[None, :]).astype(BF)
        picked = jnp.dot(pick, returned, preferred_element_type=F32)
        layer_out = layer_out + picked * route_weights[0][:, k : k + 1]
    return layer_out.astype(BF).reshape(residual.shape)


def solution(mesh):
    placed = (
        P("expert", None, "head"),
        P("expert", None, "head"),
        P("expert", None, "head"),
        P("expert", None, "head"),
        P("expert", None),
        P("head", "expert"),
        P("expert", "head", None),
        P(),
        P("expert", "head", None),
        P("expert", "head", None),
        P("head", None, "expert"),
        P("head", None, "expert"),
        P("head", "expert", None),
    )
    return jax.shard_map(
        per_device, mesh=mesh, in_specs=placed, out_specs=P("expert", "head", None), check_vma=False
    )
```

profile of v0, /device:TPU:1, one launch (start us, length us, event | category | flops | bytes accessed | tf_op | source)
XLA Modules:
  0.0 248.4 jit_solution(4226384057524479182)
XLA Ops:
  7.9 2.9 %shard_map.154 = bf16[128,768]{1,0:T(8,128)(2,1)} custom-call(s32[1]{0:T(128)} %bitcast.1.first_head, s32[1,8]{1,0:T(1,128)S(1)} %copy-done.2, bf16[128,768]{1,0:T(8,128)(2,1)} %bitcast.77, bf16[128,128]{1,0:T(8,128)(2,1)} %bitcast.82, bf16[128,128]{1,0:T(8,128)(2,1)} %bitcast.83, bf16[128,768]{1,0:T(8,128)(2,1)} %bitcast.78), custom_call_target="tpu_custom_call" | custom-call | flops 50331648 | bytes 1048576 | tf_op jit(solution)/shard_map/pallas_call | solution.py:396
  10.8 5.8 %all-to-all-start = ((bf16[8,16,768]{2,1,0:T(8,128)(2,1)}), bf16[8,16,768]{2,1,0:T(8,128)(2,1)S(1)}, u32[]{:S(2)}, u32[]{:S(2)}) async-start(bf16[8,16,768]{2,1,0:T(8,128)(2,1)} %bitcast.6), calls=%async_computation | async-start | bytes 393216 | tf_op jit(solution)/shard_map/all_to_all | solution.py:444
  17.7 4.8 %all-to-all-done = bf16[8,16,768]{2,1,0:T(8,128)(2,1)S(1)} async-done(((bf16[8,16,768]{2,1,0:T(8,128)(2,1)}), bf16[8,16,768]{2,1,0:T(8,128)(2,1)S(1)}, u32[]{:S(2)}, u32[]{:S(2)}) %all-to-all-start) | async-done | bytes 196640 | tf_op jit(solution)/shard_map/all_to_all | solution.py:444
  24.0 2.7 %collective-permute-start.2 = (bf16[8,16,768]{2,1,0:T(8,128)(2,1)S(1)}, bf16[8,16,768]{2,1,0:T(8,128)(2,1)S(1)}, u32[]{:S(2)}, u32[]{:S(2)}) collective-permute-start(bf16[8,16,768]{2,1,0:T(8,128)(2,1)S(1)} %all-to-all-done), channel_id=1, source_target_pairs={{0,8},{1,9},{2,10},{3,11},{4,12},{5,13},{6,14},{7,15},{8,0},{9,1},... | collective-permute-start | bytes 589832 | tf_op jit(solution)/shard_map/ppermute | solution.py:32
  28.5 5.4 %all-to-all-start.1 = ((bf16[16,16,512]{2,1,0:T(8,128)(2,1)}), bf16[16,16,512]{2,1,0:T(8,128)(2,1)S(1)}, u32[]{:S(2)}, u32[]{:S(2)}) async-start(bf16[16,16,512]{2,1,0:T(8,128)(2,1)} %pad_maximum_fusion.5), calls=%async_computation.1 | async-start | bytes 524288 | tf_op jit(solution)/shard_map/all_to_all | solution.py:463
  40.7 4.3 %collective-permute-done.6.refs_5_ = bf16[2,8,16,768]{3,2,1,0:T(8,128)(2,1)S(1)} collective-permute-done((bf16[2,8,16,768]{3,2,1,0:T(8,128)(2,1)S(1)}, bf16[2,8,16,768]{3,2,1,0:T(8,128)(2,1)S(1)}, u32[]{:S(2)}, u32[]{:S(2)}) %collective-permute-start.6) | collective-permute-done | bytes 393248 | tf_op jit(solution)/shard_map/ppermute | solution.py:32
  49.2 4.1 %collective-permute-done.8.refs_7_ = bf16[2,8,16,768]{3,2,1,0:T(8,128)(2,1)S(1)} collective-permute-done((bf16[2,8,16,768]{3,2,1,0:T(8,128)(2,1)S(1)}, bf16[2,8,16,768]{3,2,1,0:T(8,128)(2,1)S(1)}, u32[]{:S(2)}, u32[]{:S(2)}) %collective-permute-start.8) | collective-permute-done | bytes 393248 | tf_op jit(solution)/shard_map/ppermute | solution.py:32
  57.7 2.8 %shard_map.155 = (bf16[16,16,384]{2,1,0:T(8,128)(2,1)S(1)}, bf16[768,384]{1,0:T(8,128)(2,1)S(1)}) custom-call(s32[16]{0:T(128)S(1)} %select_reduce_fusion.place, bf16[2,8,16,768]{3,2,1,0:T(8,128)(2,1)S(1)} %pad_maximum_fusion.3.refs_0_, bf16[2,8,16,768]{3,2,1,0:T(8,128)(2,1)S(1)} %pad_maximum_fusion.4.refs_1_, ...), custom_call_target="tpu_custom_call" | custom-call | flops 1207959552 | bytes 10485760 | tf_op jit(solution)/shard_map/pallas_call | solution.py:94
  60.5 15.1 %all_to_all.25 = bf16[8,96,384]{2,1,0:T(8,128)(2,1)S(1)} all-to-all(bf16[8,96,384]{2,1,0:T(8,128)(2,1)S(1)} %bitcast.53), channel_id=1, replica_groups=mesh['head'=8,'expert'=16] {'head'}, dimensions={0} | all-to-all | bytes 1179648 | tf_op jit(solution)/shard_map/all_to_all | solution.py:483
  75.6 2.7 %collective-permute-start.11 = (bf16[768,384]{1,0:T(8,128)(2,1)S(1)}, bf16[768,384]{1,0:T(8,128)(2,1)S(1)}, u32[]{:S(2)}, u32[]{:S(2)}) collective-permute-start(bf16[768,384]{1,0:T(8,128)(2,1)S(1)} %bitcast.67), channel_id=1, source_target_pairs={{0,12},{1,13},{2,14},{3,15},{4,0},{5,1},{6,2},{7,3},{8,4},{9,5},{1... | collective-permute-start | bytes 1769480 | tf_op jit(solution)/shard_map/ppermute | solution.py:32
  78.2 4.5 %all-to-all-start.3 = ((bf16[16,16,384]{2,1,0:T(8,128)(2,1)}), bf16[16,16,384]{2,1,0:T(8,128)(2,1)S(1)}, u32[]{:S(2)}, u32[]{:S(2)}) async-start(bf16[16,16,384]{2,1,0:T(8,128)(2,1)} %copy-done.1), calls=%async_computation.3 | async-start | bytes 393216 | tf_op jit(solution)/shard_map/all_to_all | solution.py:480
  82.7 3.0 %collective-permute-done.9 = bf16[768,384]{1,0:T(8,128)(2,1)S(1)} collective-permute-done((bf16[768,384]{1,0:T(8,128)(2,1)S(1)}, bf16[768,384]{1,0:T(8,128)(2,1)S(1)}, u32[]{:S(2)}, u32[]{:S(2)}) %collective-permute-start.9) | collective-permute-done | bytes 589856 | tf_op jit(solution)/shard_map/ppermute | solution.py:32
  86.5 3.5 %collective-permute-start.12 = (bf16[384,384]{1,0:T(8,128)(2,1)S(1)}, bf16[384,384]{1,0:T(8,128)(2,1)S(1)}, u32[]{:S(2)}, u32[]{:S(2)}) collective-permute-start(bf16[384,384]{1,0:T(8,128)(2,1)S(1)} %slice.100), channel_id=1, source_target_pairs={{0,12},{1,13},{2,14},{3,15},{4,0},{5,1},{6,2},{7,3},{8,4},{9,5},{1... | collective-permute-start | bytes 884744 | tf_op jit(solution)/shard_map/ppermute | solution.py:32
  98.3 10.1 %collective-permute-done.13.refs_3_ = bf16[2,768,384]{2,1,0:T(8,128)(2,1)} collective-permute-done((bf16[2,768,384]{2,1,0:T(8,128)(2,1)}, bf16[2,768,384]{2,1,0:T(8,128)(2,1)}, u32[]{:S(2)}, u32[]{:S(2)}) %collective-permute-start.13) | collective-permute-done | bytes 1179680 | tf_op jit(solution)/shard_map/ppermute | solution.py:32
  109.2 9.3 %shard_map.156 = (f32[768,512]{1,0:T(8,128)}, f32[768,512]{1,0:T(8,128)}, f32[768,128]{1,0:T(8,128)}) custom-call(s32[8]{0:T(128)S(1)} %slice.82.refs_0_, bf16[2,768,384]{2,1,0:T(8,128)(2,1)} %pad_maximum_fusion.refs_1_, bf16[2,768,384]{2,1,0:T(8,128)(2,1)} %pad_maximum_fusion.1.refs_2_, bf16[2,768,384]{2,1,0:T(8,128)(2,1)} %collective-permute-done.13.refs_3_, ...), custom_call_target="tpu_custom_call" | custom-call | flops 4831838208 | bytes 11010048 | tf_op jit(solution)/shard_map/pallas_call | solution.py:297
  121.8 3.3 %collective-permute-start.18 = (bf16[2,768,384]{2,1,0:T(8,128)(2,1)S(1)}, bf16[2,768,384]{2,1,0:T(8,128)(2,1)}, u32[]{:S(2)}, u32[]{:S(2)}) collective-permute-start(bf16[2,768,384]{2,1,0:T(8,128)(2,1)S(1)} %collective-permute-done.16.refs_2_), channel_id=1, source_target_pairs={{0,3},{1,0},{2,1},{3,2},{4,7},{5,4},{6,5},{7,6},{8,11},{9,8},{10,9... | collective-permute-start | bytes 3538952 | tf_op jit(solution)/shard_map/ppermute | solution.py:32
  125.7 7.0 %shard_map.157 = (f32[768,512]{1,0:T(8,128)}, f32[768,512]{1,0:T(8,128)}, f32[768,128]{1,0:T(8,128)}) custom-call(s32[4]{0:T(128)S(1)} %slice.84.refs_0_, bf16[2,768,384]{2,1,0:T(8,128)(2,1)} %collective-permute-done.15.refs_1_, bf16[2,768,384]{2,1,0:T(8,128)(2,1)S(1)} %collective-permute-done.16.refs_2_, bf16[16,384,512]{2,1,0:T(8,128)(2,1)} %bitcast.59, ...), custom_call_target="tpu_custom_call" | custom-call | flops 2415919104 | bytes 5505024 | tf_op jit(solution)/shard_map/pallas_call | solution.py:297
  133.6 4.7 %collective-permute-done.18.refs_2_ = bf16[2,768,384]{2,1,0:T(8,128)(2,1)} collective-permute-done((bf16[2,768,384]{2,1,0:T(8,128)(2,1)S(1)}, bf16[2,768,384]{2,1,0:T(8,128)(2,1)}, u32[]{:S(2)}, u32[]{:S(2)}) %collective-permute-start.18) | collective-permute-done | bytes 1179680 | tf_op jit(solution)/shard_map/ppermute | solution.py:32
  138.3 11.5 %shard_map.158 = (bf16[768,512]{1,0:T(8,128)(2,1)S(1)}, bf16[96,3072]{1,0:T(8,128)(2,1)}, bf16[96,3072]{1,0:T(8,128)(2,1)}, bf16[192,3072]{1,0:T(8,128)(2,1)}, b...) custom-call(s32[4]{0:T(128)S(1)} %slice.80.refs_0_, bf16[2,768,384]{2,1,0:T(8,128)(2,1)S(1)} %collective-permute-done.14.refs_1_, ...), custom_call_target="tpu_custom_call" | custom-call | flops 2415919104 | bytes 5505024 | tf_op jit(solution)/shard_map/pallas_call | solution.py:297
  149.8 2.7 %collective-permute-start.20 = (bf16[96,3072]{1,0:T(8,128)(2,1)}, bf16[96,3072]{1,0:T(8,128)(2,1)S(1)}, u32[]{:S(2)}, u32[]{:S(2)}) collective-permute-start(bf16[96,3072]{1,0:T(8,128)(2,1)} %get-tuple-element.62), channel_id=1, source_target_pairs={{0,12},{1,13},{2,14},{3,15},{4,0},{5,1},{6,2},{7,3},{8,4},{9,5},{1... | collective-permute-start | bytes 1769480 | tf_op jit(solution)/shard_map/ppermute | solution.py:32
  152.5 6.4 %shard_map.159 = (bf16[96,3072]{1,0:T(8,128)(2,1)}, bf16[96,3072]{1,0:T(8,128)(2,1)}, bf16[192,3072]{1,0:T(8,128)(2,1)}, bf16[192,3072]{1,0:T(8,128)(2,1)}, bf16[192,3072]{1,0:T(8,128)(2,1)}) custom-call(bf16[768,512]{1,0:T(8,128)(2,1)S(1)} %get-tuple-element.58.refs_0_, bf16[512,6144]{1,0:T(8,128)(2,1)} %bitcast.65), custom_call_target="tpu_custom_call" | custom-call | flops 2415919104 | bytes 8388608 | tf_op jit(solution)/shard_map/pallas_call | solution.py:323
  160.3 2.7 %collective-permute-start.25 = (bf16[96,3072]{1,0:T(8,128)(2,1)}, bf16[96,3072]{1,0:T(8,128)(2,1)S(1)}, u32[]{:S(2)}, u32[]{:S(2)}) collective-permute-start(bf16[96,3072]{1,0:T(8,128)(2,1)} %get-tuple-element.70), channel_id=1, source_target_pairs={{0,12},{1,13},{2,14},{3,15},{4,0},{5,1},{6,2},{7,3},{8,4},{9,5},{1... | collective-permute-start | bytes 1769480 | tf_op jit(solution)/shard_map/ppermute | solution.py:32
  163.7 2.7 %collective-permute-start.22 = (bf16[192,3072]{1,0:T(8,128)(2,1)S(1)}, bf16[192,3072]{1,0:T(8,128)(2,1)S(1)}, u32[]{:S(2)}, u32[]{:S(2)}) collective-permute-start(bf16[192,3072]{1,0:T(8,128)(2,1)S(1)} %fusion.6), channel_id=1, source_target_pairs={{0,12},{1,13},{2,14},{3,15},{4,0},{5,1},{6,2},{7,3},{8,4},{9,5},{1... | collective-permute-start | bytes 3538952 | tf_op jit(solution)/shard_map/ppermute | solution.py:32
  166.4 4.3 %collective-permute-done.23 = bf16[96,3072]{1,0:T(8,128)(2,1)S(1)} collective-permute-done((bf16[96,3072]{1,0:T(8,128)(2,1)}, bf16[96,3072]{1,0:T(8,128)(2,1)S(1)}, u32[]{:S(2)}, u32[]{:S(2)}) %collective-permute-start.23) | collective-permute-done | bytes 589856 | tf_op jit(solution)/shard_map/ppermute | solution.py:32
  171.5 2.7 %collective-permute-start.26 = (bf16[192,3072]{1,0:T(8,128)(2,1)S(1)}, bf16[192,3072]{1,0:T(8,128)(2,1)S(1)}, u32[]{:S(2)}, u32[]{:S(2)}) collective-permute-start(bf16[192,3072]{1,0:T(8,128)(2,1)S(1)} %fusion.8), channel_id=1, source_target_pairs={{0,12},{1,13},{2,14},{3,15},{4,0},{5,1},{6,2},{7,3},{8,4},{9,5},{1... | collective-permute-start | bytes 3538952 | tf_op jit(solution)/shard_map/ppermute | solution.py:32
  174.2 9.2 %collective-permute-done.21 = bf16[192,3072]{1,0:T(8,128)(2,1)S(1)} collective-permute-done((bf16[192,3072]{1,0:T(8,128)(2,1)S(1)}, bf16[192,3072]{1,0:T(8,128)(2,1)S(1)}, u32[]{:S(2)}, u32[]{:S(2)}) %collective-permute-start.21) | collective-permute-done | bytes 1179680 | tf_op jit(solution)/shard_map/ppermute | solution.py:32
  184.0 12.0 %collective-permute-done.24 = bf16[192,3072]{1,0:T(8,128)(2,1)S(1)} collective-permute-done((bf16[192,3072]{1,0:T(8,128)(2,1)S(1)}, bf16[192,3072]{1,0:T(8,128)(2,1)S(1)}, u32[]{:S(2)}, u32[]{:S(2)}) %collective-permute-start.24) | collective-permute-done | bytes 1179680 | tf_op jit(solution)/shard_map/ppermute | solution.py:32
  199.0 2.6 %collective-permute-start.28 = (bf16[48,6144]{1,0:T(8,128)(2,1)}, bf16[48,6144]{1,0:T(8,128)(2,1)}, u32[]{:S(2)}, u32[]{:S(2)}) collective-permute-start(bf16[48,6144]{1,0:T(8,128)(2,1)} %get-tuple-element.81), channel_id=1, source_target_pairs={{0,1},{1,2},{2,3},{3,0},{4,5},{5,6},{6,7},{7,4},{8,9},{9,10},{10,1... | collective-permute-start | bytes 1769480 | tf_op jit(solution)/shard_map/ppermute | solution.py:32
  201.7 7.0 %collective-permute-done.27 = bf16[48,6144]{1,0:T(8,128)(2,1)} collective-permute-done((bf16[48,6144]{1,0:T(8,128)(2,1)}, bf16[48,6144]{1,0:T(8,128)(2,1)}, u32[]{:S(2)}, u32[]{:S(2)}) %collective-permute-start.27) | collective-permute-done | bytes 589856 | tf_op jit(solution)/shard_map/ppermute | solution.py:32
  208.7 6.3 %collective-permute-done.28 = bf16[48,6144]{1,0:T(8,128)(2,1)} collective-permute-done((bf16[48,6144]{1,0:T(8,128)(2,1)}, bf16[48,6144]{1,0:T(8,128)(2,1)}, u32[]{:S(2)}, u32[]{:S(2)}) %collective-permute-start.28) | collective-permute-done | bytes 589856 | tf_op jit(solution)/shard_map/ppermute | solution.py:32
  218.7 9.1 %all-to-all-start.4 = ((bf16[8,6,6144]{2,1,0:T(8,128)(2,1)}), bf16[8,6,6144]{2,1,0:T(8,128)(2,1)S(1)}, u32[]{:S(2)}, u32[]{:S(2)}) async-start(bf16[8,6,6144]{2,1,0:T(8,128)(2,1)} %reshape.174), calls=%async_computation.4 | async-start | bytes 1572864 | tf_op jit(solution)/shard_map/all_to_all | solution.py:524
  228.1 12.0 %all-to-all-done.4 = bf16[8,6,6144]{2,1,0:T(8,128)(2,1)S(1)} async-done(((bf16[8,6,6144]{2,1,0:T(8,128)(2,1)}), bf16[8,6,6144]{2,1,0:T(8,128)(2,1)S(1)}, u32[]{:S(2)}, u32[]{:S(2)}) %all-to-all-start.4) | async-done | bytes 589856 | tf_op jit(solution)/shard_map/all_to_all | solution.py:524
  (147 shorter events, 47.2 us)
Async XLA Ops:
  6.5 40.7 %all-gather.3.cloned.1.call-start = ((), (), s32[]{:S(2)}) async-start(), calls=%async_computation.5 | async-start | bytes 5308416 | tf_op jit(solution)/shard_map/all_gather | solution.py:441
  10.8 11.7 %all-to-all-start = ((bf16[8,16,768]{2,1,0:T(8,128)(2,1)}), bf16[8,16,768]{2,1,0:T(8,128)(2,1)S(1)}, u32[]{:S(2)}, u32[]{:S(2)}) async-start(bf16[8,16,768]{2,1,0:T(8,128)(2,1)} %bitcast.6), calls=%async_computation | async-start | bytes 393216 | tf_op jit(solution)/shard_map/all_to_all | solution.py:444
  22.5 11.5 %collective-permute-start = (bf16[8,16,768]{2,1,0:T(8,128)(2,1)S(1)}, bf16[8,16,768]{2,1,0:T(8,128)(2,1)S(1)}, u32[]{:S(2)}, u32[]{:S(2)}) collective-permute-start(bf16[8,16,768]{2,1,0:T(8,128)(2,1)S(1)} %all-to-all-done), channel_id=1, source_target_pairs={{0,4},{1,5},{2,6},{3,7},{4,8},{5,9},{6,10},{7,11},{8,12},{9,13},{1... | collective-permute-start | bytes 589832 | tf_op jit(solution)/shard_map/ppermute | solution.py:32
  24.0 11.4 %collective-permute-start.2 = (bf16[8,16,768]{2,1,0:T(8,128)(2,1)S(1)}, bf16[8,16,768]{2,1,0:T(8,128)(2,1)S(1)}, u32[]{:S(2)}, u32[]{:S(2)}) collective-permute-start(bf16[8,16,768]{2,1,0:T(8,128)(2,1)S(1)} %all-to-all-done), channel_id=1, source_target_pairs={{0,8},{1,9},{2,10},{3,11},{4,12},{5,13},{6,14},{7,15},{8,0},{9,1},... | collective-permute-start | bytes 589832 | tf_op jit(solution)/shard_map/ppermute | solution.py:32
  26.7 8.7 %collective-permute-start.1 = (bf16[8,16,768]{2,1,0:T(8,128)(2,1)S(1)}, bf16[8,16,768]{2,1,0:T(8,128)(2,1)S(1)}, u32[]{:S(2)}, u32[]{:S(2)}) collective-permute-start(bf16[8,16,768]{2,1,0:T(8,128)(2,1)S(1)} %all-to-all-done), channel_id=1, source_target_pairs={{0,12},{1,13},{2,14},{3,15},{4,0},{5,1},{6,2},{7,3},{8,4},{9,5},{1... | collective-permute-start | bytes 589832 | tf_op jit(solution)/shard_map/ppermute | solution.py:32
  28.5 19.7 %all-to-all-start.1 = ((bf16[16,16,512]{2,1,0:T(8,128)(2,1)}), bf16[16,16,512]{2,1,0:T(8,128)(2,1)S(1)}, u32[]{:S(2)}, u32[]{:S(2)}) async-start(bf16[16,16,512]{2,1,0:T(8,128)(2,1)} %pad_maximum_fusion.5), calls=%async_computation.1 | async-start | bytes 524288 | tf_op jit(solution)/shard_map/all_to_all | solution.py:463
  34.0 13.2 %collective-permute-start.3 = (bf16[2,8,16,768]{3,2,1,0:T(8,128)(2,1)S(1)}, bf16[2,8,16,768]{3,2,1,0:T(8,128)(2,1)S(1)}, u32[]{:S(2)}, u32[]{:S(2)}) collective-permute-start(bf16[2,8,16,768]{3,2,1,0:T(8,128)(2,1)S(1)} %pad_maximum_fusion.3.refs_0_), channel_id=1, source_target_pairs={{0,1},{1,2},{2,3},{3,0},{4,5},{5,6},{6,7},{7,4},{8,9},{9,10},{10,1... | collective-permute-start | bytes 1179656 | tf_op jit(solution)/shard_map/ppermute | solution.py:32
  35.5 9.6 %collective-permute-start.6 = (bf16[2,8,16,768]{3,2,1,0:T(8,128)(2,1)S(1)}, bf16[2,8,16,768]{3,2,1,0:T(8,128)(2,1)S(1)}, u32[]{:S(2)}, u32[]{:S(2)}) collective-permute-start(bf16[2,8,16,768]{3,2,1,0:T(8,128)(2,1)S(1)} %pad_maximum_fusion.4.refs_1_), channel_id=1, source_target_pairs={{0,3},{1,0},{2,1},{3,2},{4,7},{5,4},{6,5},{7,6},{8,11},{9,8},{10,9... | collective-permute-start | bytes 1179656 | tf_op jit(solution)/shard_map/ppermute | solution.py:32
  38.0 11.2 %collective-permute-start.5 = (bf16[2,8,16,768]{3,2,1,0:T(8,128)(2,1)S(1)}, bf16[2,8,16,768]{3,2,1,0:T(8,128)(2,1)S(1)}, u32[]{:S(2)}, u32[]{:S(2)}) collective-permute-start(bf16[2,8,16,768]{3,2,1,0:T(8,128)(2,1)S(1)} %pad_maximum_fusion.4.refs_1_), channel_id=1, source_target_pairs={{0,1},{1,2},{2,3},{3,0},{4,5},{5,6},{6,7},{7,4},{8,9},{9,10},{10,1... | collective-permute-start | bytes 1179656 | tf_op jit(solution)/shard_map/ppermute | solution.py:32
  38.2 11.0 %collective-permute-start.4 = (bf16[2,8,16,768]{3,2,1,0:T(8,128)(2,1)S(1)}, bf16[2,8,16,768]{3,2,1,0:T(8,128)(2,1)S(1)}, u32[]{:S(2)}, u32[]{:S(2)}) collective-permute-start(bf16[2,8,16,768]{3,2,1,0:T(8,128)(2,1)S(1)} %pad_maximum_fusion.3.refs_0_), channel_id=1, source_target_pairs={{0,3},{1,0},{2,1},{3,2},{4,7},{5,4},{6,5},{7,6},{8,11},{9,8},{10,9... | collective-permute-start | bytes 1179656 | tf_op jit(solution)/shard_map/ppermute | solution.py:32
  75.5 10.2 %collective-permute-start.9 = (bf16[768,384]{1,0:T(8,128)(2,1)S(1)}, bf16[768,384]{1,0:T(8,128)(2,1)S(1)}, u32[]{:S(2)}, u32[]{:S(2)}) collective-permute-start(bf16[768,384]{1,0:T(8,128)(2,1)S(1)} %bitcast.66), channel_id=1, source_target_pairs={{0,4},{1,5},{2,6},{3,7},{4,8},{5,9},{6,10},{7,11},{8,12},{9,13},{1... | collective-permute-start | bytes 1769480 | tf_op jit(solution)/shard_map/ppermute | solution.py:32
  75.6 11.0 %collective-permute-start.11 = (bf16[768,384]{1,0:T(8,128)(2,1)S(1)}, bf16[768,384]{1,0:T(8,128)(2,1)S(1)}, u32[]{:S(2)}, u32[]{:S(2)}) collective-permute-start(bf16[768,384]{1,0:T(8,128)(2,1)S(1)} %bitcast.67), channel_id=1, source_target_pairs={{0,12},{1,13},{2,14},{3,15},{4,0},{5,1},{6,2},{7,3},{8,4},{9,5},{1... | collective-permute-start | bytes 1769480 | tf_op jit(solution)/shard_map/ppermute | solution.py:32
  78.2 16.0 %all-to-all-start.3 = ((bf16[16,16,384]{2,1,0:T(8,128)(2,1)}), bf16[16,16,384]{2,1,0:T(8,128)(2,1)S(1)}, u32[]{:S(2)}, u32[]{:S(2)}) async-start(bf16[16,16,384]{2,1,0:T(8,128)(2,1)} %copy-done.1), calls=%async_computation.3 | async-start | bytes 393216 | tf_op jit(solution)/shard_map/all_to_all | solution.py:480
  85.8 8.4 %collective-permute-start.10 = (bf16[384,384]{1,0:T(8,128)(2,1)S(1)}, bf16[384,384]{1,0:T(8,128)(2,1)S(1)}, u32[]{:S(2)}, u32[]{:S(2)}) collective-permute-start(bf16[384,384]{1,0:T(8,128)(2,1)S(1)} %slice.99), channel_id=1, source_target_pairs={{0,4},{1,5},{2,6},{3,7},{4,8},{5,9},{6,10},{7,11},{8,12},{9,13},{1... | collective-permute-start | bytes 884744 | tf_op jit(solution)/shard_map/ppermute | solution.py:32
  91.3 17.1 %collective-permute-start.13 = (bf16[2,768,384]{2,1,0:T(8,128)(2,1)}, bf16[2,768,384]{2,1,0:T(8,128)(2,1)}, u32[]{:S(2)}, u32[]{:S(2)}) collective-permute-start(bf16[2,768,384]{2,1,0:T(8,128)(2,1)} %pad_maximum_fusion.refs_1_), channel_id=1, source_target_pairs={{0,1},{1,2},{2,3},{3,0},{4,5},{5,6},{6,7},{7,4},{8,9},{9,10},{10,1... | collective-permute-start | bytes 3538952 | tf_op jit(solution)/shard_map/ppermute | solution.py:32
  93.0 16.2 %collective-permute-start.17 = (bf16[2,768,384]{2,1,0:T(8,128)(2,1)}, bf16[2,768,384]{2,1,0:T(8,128)(2,1)}, u32[]{:S(2)}, u32[]{:S(2)}) collective-permute-start(bf16[2,768,384]{2,1,0:T(8,128)(2,1)} %pad_maximum_fusion.refs_1_), channel_id=1, source_target_pairs={{0,3},{1,0},{2,1},{3,2},{4,7},{5,4},{6,5},{7,6},{8,11},{9,8},{10,9... | collective-permute-start | bytes 3538952 | tf_op jit(solution)/shard_map/ppermute | solution.py:32
  95.5 25.5 %collective-permute-start.15 = (bf16[2,768,384]{2,1,0:T(8,128)(2,1)}, bf16[2,768,384]{2,1,0:T(8,128)(2,1)}, u32[]{:S(2)}, u32[]{:S(2)}) collective-permute-start(bf16[2,768,384]{2,1,0:T(8,128)(2,1)} %pad_maximum_fusion.1.refs_2_), channel_id=1, source_target_pairs={{0,1},{1,2},{2,3},{3,0},{4,5},{5,6},{6,7},{7,4},{8,9},{9,10},{10,1... | collective-permute-start | bytes 3538952 | tf_op jit(solution)/shard_map/ppermute | solution.py:32
  96.7 25.1 %collective-permute-start.16 = (bf16[2,768,384]{2,1,0:T(8,128)(2,1)}, bf16[2,768,384]{2,1,0:T(8,128)(2,1)S(1)}, u32[]{:S(2)}, u32[]{:S(2)}) collective-permute-start(bf16[2,768,384]{2,1,0:T(8,128)(2,1)} %pad_maximum_fusion.1.refs_2_), channel_id=1, source_target_pairs={{0,3},{1,0},{2,1},{3,2},{4,7},{5,4},{6,5},{7,6},{8,11},{9,8},{10,9... | collective-permute-start | bytes 3538952 | tf_op jit(solution)/shard_map/ppermute | solution.py:32
  108.4 25.2 %collective-permute-start.14 = (bf16[2,768,384]{2,1,0:T(8,128)(2,1)}, bf16[2,768,384]{2,1,0:T(8,128)(2,1)S(1)}, u32[]{:S(2)}, u32[]{:S(2)}) collective-permute-start(bf16[2,768,384]{2,1,0:T(8,128)(2,1)} %collective-permute-done.13.refs_3_), channel_id=1, source_target_pairs={{0,1},{1,2},{2,3},{3,0},{4,5},{5,6},{6,7},{7,4},{8,9},{9,10},{10,1... | collective-permute-start | bytes 3538952 | tf_op jit(solution)/shard_map/ppermute | solution.py:32
  121.8 16.5 %collective-permute-start.18 = (bf16[2,768,384]{2,1,0:T(8,128)(2,1)S(1)}, bf16[2,768,384]{2,1,0:T(8,128)(2,1)}, u32[]{:S(2)}, u32[]{:S(2)}) collective-permute-start(bf16[2,768,384]{2,1,0:T(8,128)(2,1)S(1)} %collective-permute-done.16.refs_2_), channel_id=1, source_target_pairs={{0,3},{1,0},{2,1},{3,2},{4,7},{5,4},{6,5},{7,6},{8,11},{9,8},{10,9... | collective-permute-start | bytes 3538952 | tf_op jit(solution)/shard_map/ppermute | solution.py:32
  149.8 10.5 %collective-permute-start.19 = (bf16[96,3072]{1,0:T(8,128)(2,1)}, bf16[96,3072]{1,0:T(8,128)(2,1)S(1)}, u32[]{:S(2)}, u32[]{:S(2)}) collective-permute-start(bf16[96,3072]{1,0:T(8,128)(2,1)} %get-tuple-element.61), channel_id=1, source_target_pairs={{0,4},{1,5},{2,6},{3,7},{4,8},{5,9},{6,10},{7,11},{8,12},{9,13},{1... | collective-permute-start | bytes 1769480 | tf_op jit(solution)/shard_map/ppermute | solution.py:32
  149.8 10.4 %collective-permute-start.20 = (bf16[96,3072]{1,0:T(8,128)(2,1)}, bf16[96,3072]{1,0:T(8,128)(2,1)S(1)}, u32[]{:S(2)}, u32[]{:S(2)}) collective-permute-start(bf16[96,3072]{1,0:T(8,128)(2,1)} %get-tuple-element.62), channel_id=1, source_target_pairs={{0,12},{1,13},{2,14},{3,15},{4,0},{5,1},{6,2},{7,3},{8,4},{9,5},{1... | collective-permute-start | bytes 1769480 | tf_op jit(solution)/shard_map/ppermute | solution.py:32
  160.3 10.5 %collective-permute-start.23 = (bf16[96,3072]{1,0:T(8,128)(2,1)}, bf16[96,3072]{1,0:T(8,128)(2,1)S(1)}, u32[]{:S(2)}, u32[]{:S(2)}) collective-permute-start(bf16[96,3072]{1,0:T(8,128)(2,1)} %get-tuple-element.68), channel_id=1, source_target_pairs={{0,4},{1,5},{2,6},{3,7},{4,8},{5,9},{6,10},{7,11},{8,12},{9,13},{1... | collective-permute-start | bytes 1769480 | tf_op jit(solution)/shard_map/ppermute | solution.py:32
  160.3 10.9 %collective-permute-start.25 = (bf16[96,3072]{1,0:T(8,128)(2,1)}, bf16[96,3072]{1,0:T(8,128)(2,1)S(1)}, u32[]{:S(2)}, u32[]{:S(2)}) collective-permute-start(bf16[96,3072]{1,0:T(8,128)(2,1)} %get-tuple-element.70), channel_id=1, source_target_pairs={{0,12},{1,13},{2,14},{3,15},{4,0},{5,1},{6,2},{7,3},{8,4},{9,5},{1... | collective-permute-start | bytes 1769480 | tf_op jit(solution)/shard_map/ppermute | solution.py:32
  163.3 20.1 %collective-permute-start.21 = (bf16[192,3072]{1,0:T(8,128)(2,1)S(1)}, bf16[192,3072]{1,0:T(8,128)(2,1)S(1)}, u32[]{:S(2)}, u32[]{:S(2)}) collective-permute-start(bf16[192,3072]{1,0:T(8,128)(2,1)S(1)} %fusion.5), channel_id=1, source_target_pairs={{0,4},{1,5},{2,6},{3,7},{4,8},{5,9},{6,10},{7,11},{8,12},{9,13},{1... | collective-permute-start | bytes 3538952 | tf_op jit(solution)/shard_map/ppermute | solution.py:32
  163.7 19.7 %collective-permute-start.22 = (bf16[192,3072]{1,0:T(8,128)(2,1)S(1)}, bf16[192,3072]{1,0:T(8,128)(2,1)S(1)}, u32[]{:S(2)}, u32[]{:S(2)}) collective-permute-start(bf16[192,3072]{1,0:T(8,128)(2,1)S(1)} %fusion.6), channel_id=1, source_target_pairs={{0,12},{1,13},{2,14},{3,15},{4,0},{5,1},{6,2},{7,3},{8,4},{9,5},{1... | collective-permute-start | bytes 3538952 | tf_op jit(solution)/shard_map/ppermute | solution.py:32
  171.1 24.9 %collective-permute-start.24 = (bf16[192,3072]{1,0:T(8,128)(2,1)S(1)}, bf16[192,3072]{1,0:T(8,128)(2,1)S(1)}, u32[]{:S(2)}, u32[]{:S(2)}) collective-permute-start(bf16[192,3072]{1,0:T(8,128)(2,1)S(1)} %fusion.7), channel_id=1, source_target_pairs={{0,4},{1,5},{2,6},{3,7},{4,8},{5,9},{6,10},{7,11},{8,12},{9,13},{1... | collective-permute-start | bytes 3538952 | tf_op jit(solution)/shard_map/ppermute | solution.py:32
  171.5 24.5 %collective-permute-start.26 = (bf16[192,3072]{1,0:T(8,128)(2,1)S(1)}, bf16[192,3072]{1,0:T(8,128)(2,1)S(1)}, u32[]{:S(2)}, u32[]{:S(2)}) collective-permute-start(bf16[192,3072]{1,0:T(8,128)(2,1)S(1)} %fusion.8), channel_id=1, source_target_pairs={{0,12},{1,13},{2,14},{3,15},{4,0},{5,1},{6,2},{7,3},{8,4},{9,5},{1... | collective-permute-start | bytes 3538952 | tf_op jit(solution)/shard_map/ppermute | solution.py:32
  197.8 10.9 %collective-permute-start.27 = (bf16[48,6144]{1,0:T(8,128)(2,1)}, bf16[48,6144]{1,0:T(8,128)(2,1)}, u32[]{:S(2)}, u32[]{:S(2)}) collective-permute-start(bf16[48,6144]{1,0:T(8,128)(2,1)} %get-tuple-element.79), channel_id=1, source_target_pairs={{0,2},{1,3},{2,0},{3,1},{4,6},{5,7},{6,4},{7,5},{8,10},{9,11},{10,... | collective-permute-start | bytes 1769480 | tf_op jit(solution)/shard_map/ppermute | solution.py:32
  199.0 16.0 %collective-permute-start.28 = (bf16[48,6144]{1,0:T(8,128)(2,1)}, bf16[48,6144]{1,0:T(8,128)(2,1)}, u32[]{:S(2)}, u32[]{:S(2)}) collective-permute-start(bf16[48,6144]{1,0:T(8,128)(2,1)} %get-tuple-element.81), channel_id=1, source_target_pairs={{0,1},{1,2},{2,3},{3,0},{4,5},{5,6},{6,7},{7,4},{8,9},{9,10},{10,1... | collective-permute-start | bytes 1769480 | tf_op jit(solution)/shard_map/ppermute | solution.py:32
  201.6 14.2 %collective-permute-start.29 = (bf16[48,6144]{1,0:T(8,128)(2,1)S(1)}, bf16[48,6144]{1,0:T(8,128)(2,1)}, u32[]{:S(2)}, u32[]{:S(2)}) collective-permute-start(bf16[48,6144]{1,0:T(8,128)(2,1)S(1)} %get-tuple-element.80), channel_id=1, source_target_pairs={{0,3},{1,0},{2,1},{3,2},{4,7},{5,4},{6,5},{7,6},{8,11},{9,8},{10,9... | collective-permute-start | bytes 1769480 | tf_op jit(solution)/shard_map/ppermute | solution.py:32
  218.7 21.4 %all-to-all-start.4 = ((bf16[8,6,6144]{2,1,0:T(8,128)(2,1)}), bf16[8,6,6144]{2,1,0:T(8,128)(2,1)S(1)}, u32[]{:S(2)}, u32[]{:S(2)}) async-start(bf16[8,6,6144]{2,1,0:T(8,128)(2,1)} %reshape.174), calls=%async_computation.4 | async-start | bytes 1572864 | tf_op jit(solution)/shard_map/all_to_all | solution.py:524
  (23 other events, 208.3 us)
Sparse Core Ops, SparseCore 0:
  9.0 37.8 all-gather.2
where the time goes:
time: 249 us; the launch traced here: 248 us
  waiting for transfers between devices  92.8 us (37%)
  starting transfers between devices  68.9 us (28%)
  Pallas kernels  39.9 us (16%)
  blocking collectives  15.1 us (6%)
  between operations  13.9 us (6%)
  other arithmetic  9.82 us (4%)
  local copies, waits for them, and re-layouts  6.61 us (3%)
    ppermute x30, waiting for transfers between devices, send(): return lax.ppermute(block, ('head', 'expert'), ring_pairs(near, step))  75.2 us
    ppermute x30, starting transfers between devices, send(): return lax.ppermute(block, ('head', 'expert'), ring_pairs(near, step))  44.1 us
    pallas_call x3, Pallas kernels, gate_up(): pl.pallas_call(lambda *refs: gate_up_kernel(shapes, finish, begun, len(pr...  27.8 us
    all_to_all x1, blocking collectives, per_device(): lax.all_to_all(slots, 'head', split_axis=0, concat_axis=0, tiled=True)  15.1 us
    all_to_all x1, waiting for transfers between devices, per_device(): lax.all_to_all(totals, 'head', split_axis=0, concat_axis=0, tiled=True)  12 us
    all_to_all x1, starting transfers between devices, per_device(): lax.all_to_all(totals, 'head', split_axis=0, concat_axis=0, tiled=True)  9.09 us
    pallas_call x1, Pallas kernels, down(): pl.pallas_call(lambda *refs: down_kernel(start, *refs), out_shape=[pltpu....  6.44 us
    all_to_all x1, starting transfers between devices, per_device(): lax.all_to_all(merged, 'head', split_axis=0, concat_axis=0, tiled=True)  5.81 us
  transfers between devices with their start and end apart: 35, of which 21 were waited for; matrix products, arithmetic and copies ran while one was open for 3% of the time, Pallas kernels for 10%

commit v1 on v0

--- a/solution.py
+++ b/solution.py
@@ -110,7 +110,7 @@
     )(place, *blocks, weight, resid, gain, targets)
 
 
-DOWN_STEP = 768
+DOWN_STEP = 1536
 
 
 def down_scratch(rows, depth, wide, parts):

time: 249 us -> 248 us (level)
  transfers between devices with their start and end apart: 35 -> 35, of which waited for: 21 -> 21; matrix products, arithmetic and copies ran while one was open for 3% -> 4% of each run, Pallas kernels for 10% -> 10%
where the time goes in v1:
time: 248 us
  waiting for transfers between devices  93.3 us (38%)
  starting transfers between devices  69.1 us (28%)
  Pallas kernels  38.5 us (16%)
  blocking collectives  15.1 us (6%)
  between operations  13.9 us (6%)
  other arithmetic  9.82 us (4%)
  local copies, waits for them, and re-layouts  6.61 us (3%)
    ppermute x30, waiting for transfers between devices, send(): return lax.ppermute(block, ('head', 'expert'), ring_pairs(near, step))  75.7 us
    ppermute x30, starting transfers between devices, send(): return lax.ppermute(block, ('head', 'expert'), ring_pairs(near, step))  44.3 us
    pallas_call x3, Pallas kernels, gate_up(): pl.pallas_call(lambda *refs: gate_up_kernel(shapes, finish, begun, len(pr...  26.9 us
    all_to_all x1, blocking collectives, per_device(): lax.all_to_all(slots, 'head', split_axis=0, concat_axis=0, tiled=True)  15.1 us
    all_to_all x1, waiting for transfers between devices, per_device(): lax.all_to_all(totals, 'head', split_axis=0, concat_axis=0, tiled=True)  12 us
    all_to_all x1, starting transfers between devices, per_device(): lax.all_to_all(totals, 'head', split_axis=0, concat_axis=0, tiled=True)  9.08 us
    pallas_call x1, Pallas kernels, down(): pl.pallas_call(lambda *refs: down_kernel(start, *refs), out_shape=[pltpu....  5.95 us
    all_to_all x1, starting transfers between devices, per_device(): lax.all_to_all(merged, 'head', split_axis=0, concat_axis=0, tiled=True)  5.81 us
  transfers between devices with their start and end apart: 35, of which 21 were waited for; matrix products, arithmetic and copies ran while one was open for 4% of the time, Pallas kernels for 10%

profile of v1, /device:TPU:1, one launch (start us, length us, event | category | flops | bytes accessed | tf_op | source)
XLA Modules:
  0.0 247.7 jit_solution(8036157616637692264)
XLA Ops:
  7.9 2.9 %shard_map.154 = bf16[128,768]{1,0:T(8,128)(2,1)} custom-call(s32[1]{0:T(128)} %bitcast.1.first_head, s32[1,8]{1,0:T(1,128)S(1)} %copy-done.2, bf16[128,768]{1,0:T(8,128)(2,1)} %bitcast.77, bf16[128,128]{1,0:T(8,128)(2,1)} %bitcast.82, bf16[128,128]{1,0:T(8,128)(2,1)} %bitcast.83, bf16[128,768]{1,0:T(8,128)(2,1)} %bitcast.78), custom_call_target="tpu_custom_call" | custom-call | flops 50331648 | bytes 1048576 | tf_op jit(solution)/shard_map/pallas_call | solution.py:396
  10.8 5.8 %all-to-all-start = ((bf16[8,16,768]{2,1,0:T(8,128)(2,1)}), bf16[8,16,768]{2,1,0:T(8,128)(2,1)S(1)}, u32[]{:S(2)}, u32[]{:S(2)}) async-start(bf16[8,16,768]{2,1,0:T(8,128)(2,1)} %bitcast.6), calls=%async_computation | async-start | bytes 393216 | tf_op jit(solution)/shard_map/all_to_all | solution.py:444
  17.7 4.8 %all-to-all-done = bf16[8,16,768]{2,1,0:T(8,128)(2,1)S(1)} async-done(((bf16[8,16,768]{2,1,0:T(8,128)(2,1)}), bf16[8,16,768]{2,1,0:T(8,128)(2,1)S(1)}, u32[]{:S(2)}, u32[]{:S(2)}) %all-to-all-start) | async-done | bytes 196640 | tf_op jit(solution)/shard_map/all_to_all | solution.py:444
  24.0 2.7 %collective-permute-start.2 = (bf16[8,16,768]{2,1,0:T(8,128)(2,1)S(1)}, bf16[8,16,768]{2,1,0:T(8,128)(2,1)S(1)}, u32[]{:S(2)}, u32[]{:S(2)}) collective-permute-start(bf16[8,16,768]{2,1,0:T(8,128)(2,1)S(1)} %all-to-all-done), channel_id=1, source_target_pairs={{0,8},{1,9},{2,10},{3,11},{4,12},{5,13},{6,14},{7,15},{8,0},{9,1},... | collective-permute-start | bytes 589832 | tf_op jit(solution)/shard_map/ppermute | solution.py:32
  28.5 5.4 %all-to-all-start.1 = ((bf16[16,16,512]{2,1,0:T(8,128)(2,1)}), bf16[16,16,512]{2,1,0:T(8,128)(2,1)S(1)}, u32[]{:S(2)}, u32[]{:S(2)}) async-start(bf16[16,16,512]{2,1,0:T(8,128)(2,1)} %pad_maximum_fusion.5), calls=%async_computation.1 | async-start | bytes 524288 | tf_op jit(solution)/shard_map/all_to_all | solution.py:463
  40.7 4.3 %collective-permute-done.6.refs_5_ = bf16[2,8,16,768]{3,2,1,0:T(8,128)(2,1)S(1)} collective-permute-done((bf16[2,8,16,768]{3,2,1,0:T(8,128)(2,1)S(1)}, bf16[2,8,16,768]{3,2,1,0:T(8,128)(2,1)S(1)}, u32[]{:S(2)}, u32[]{:S(2)}) %collective-permute-start.6) | collective-permute-done | bytes 393248 | tf_op jit(solution)/shard_map/ppermute | solution.py:32
  49.2 4.1 %collective-permute-done.8.refs_7_ = bf16[2,8,16,768]{3,2,1,0:T(8,128)(2,1)S(1)} collective-permute-done((bf16[2,8,16,768]{3,2,1,0:T(8,128)(2,1)S(1)}, bf16[2,8,16,768]{3,2,1,0:T(8,128)(2,1)S(1)}, u32[]{:S(2)}, u32[]{:S(2)}) %collective-permute-start.8) | collective-permute-done | bytes 393248 | tf_op jit(solution)/shard_map/ppermute | solution.py:32
  57.7 2.8 %shard_map.155 = (bf16[16,16,384]{2,1,0:T(8,128)(2,1)S(1)}, bf16[768,384]{1,0:T(8,128)(2,1)S(1)}) custom-call(s32[16]{0:T(128)S(1)} %select_reduce_fusion.place, bf16[2,8,16,768]{3,2,1,0:T(8,128)(2,1)S(1)} %pad_maximum_fusion.3.refs_0_, bf16[2,8,16,768]{3,2,1,0:T(8,128)(2,1)S(1)} %pad_maximum_fusion.4.refs_1_, ...), custom_call_target="tpu_custom_call" | custom-call | flops 1207959552 | bytes 10485760 | tf_op jit(solution)/shard_map/pallas_call | solution.py:94
  60.5 15.1 %all_to_all.25 = bf16[8,96,384]{2,1,0:T(8,128)(2,1)S(1)} all-to-all(bf16[8,96,384]{2,1,0:T(8,128)(2,1)S(1)} %bitcast.53), channel_id=1, replica_groups=mesh['head'=8,'expert'=16] {'head'}, dimensions={0} | all-to-all | bytes 1179648 | tf_op jit(solution)/shard_map/all_to_all | solution.py:483
  75.6 2.7 %collective-permute-start.11 = (bf16[768,384]{1,0:T(8,128)(2,1)S(1)}, bf16[768,384]{1,0:T(8,128)(2,1)S(1)}, u32[]{:S(2)}, u32[]{:S(2)}) collective-permute-start(bf16[768,384]{1,0:T(8,128)(2,1)S(1)} %bitcast.67), channel_id=1, source_target_pairs={{0,12},{1,13},{2,14},{3,15},{4,0},{5,1},{6,2},{7,3},{8,4},{9,5},{1... | collective-permute-start | bytes 1769480 | tf_op jit(solution)/shard_map/ppermute | solution.py:32
  78.2 4.5 %all-to-all-start.3 = ((bf16[16,16,384]{2,1,0:T(8,128)(2,1)}), bf16[16,16,384]{2,1,0:T(8,128)(2,1)S(1)}, u32[]{:S(2)}, u32[]{:S(2)}) async-start(bf16[16,16,384]{2,1,0:T(8,128)(2,1)} %copy-done.1), calls=%async_computation.3 | async-start | bytes 393216 | tf_op jit(solution)/shard_map/all_to_all | solution.py:480
  82.7 3.0 %collective-permute-done.9 = bf16[768,384]{1,0:T(8,128)(2,1)S(1)} collective-permute-done((bf16[768,384]{1,0:T(8,128)(2,1)S(1)}, bf16[768,384]{1,0:T(8,128)(2,1)S(1)}, u32[]{:S(2)}, u32[]{:S(2)}) %collective-permute-start.9) | collective-permute-done | bytes 589856 | tf_op jit(solution)/shard_map/ppermute | solution.py:32
  86.5 3.5 %collective-permute-start.12 = (bf16[384,384]{1,0:T(8,128)(2,1)S(1)}, bf16[384,384]{1,0:T(8,128)(2,1)S(1)}, u32[]{:S(2)}, u32[]{:S(2)}) collective-permute-start(bf16[384,384]{1,0:T(8,128)(2,1)S(1)} %slice.100), channel_id=1, source_target_pairs={{0,12},{1,13},{2,14},{3,15},{4,0},{5,1},{6,2},{7,3},{8,4},{9,5},{1... | collective-permute-start | bytes 884744 | tf_op jit(solution)/shard_map/ppermute | solution.py:32
  98.3 10.1 %collective-permute-done.13.refs_3_ = bf16[2,768,384]{2,1,0:T(8,128)(2,1)} collective-permute-done((bf16[2,768,384]{2,1,0:T(8,128)(2,1)}, bf16[2,768,384]{2,1,0:T(8,128)(2,1)}, u32[]{:S(2)}, u32[]{:S(2)}) %collective-permute-start.13) | collective-permute-done | bytes 1179680 | tf_op jit(solution)/shard_map/ppermute | solution.py:32
  109.2 9.3 %shard_map.156 = (f32[768,512]{1,0:T(8,128)}, f32[768,512]{1,0:T(8,128)}, f32[768,128]{1,0:T(8,128)}) custom-call(s32[8]{0:T(128)S(1)} %slice.82.refs_0_, bf16[2,768,384]{2,1,0:T(8,128)(2,1)} %pad_maximum_fusion.refs_1_, bf16[2,768,384]{2,1,0:T(8,128)(2,1)} %pad_maximum_fusion.1.refs_2_, bf16[2,768,384]{2,1,0:T(8,128)(2,1)} %collective-permute-done.13.refs_3_, ...), custom_call_target="tpu_custom_call" | custom-call | flops 4831838208 | bytes 11010048 | tf_op jit(solution)/shard_map/pallas_call | solution.py:297
  121.8 3.3 %collective-permute-start.18 = (bf16[2,768,384]{2,1,0:T(8,128)(2,1)S(1)}, bf16[2,768,384]{2,1,0:T(8,128)(2,1)}, u32[]{:S(2)}, u32[]{:S(2)}) collective-permute-start(bf16[2,768,384]{2,1,0:T(8,128)(2,1)S(1)} %collective-permute-done.16.refs_2_), channel_id=1, source_target_pairs={{0,3},{1,0},{2,1},{3,2},{4,7},{5,4},{6,5},{7,6},{8,11},{9,8},{10,9... | collective-permute-start | bytes 3538952 | tf_op jit(solution)/shard_map/ppermute | solution.py:32
  125.7 7.0 %shard_map.157 = (f32[768,512]{1,0:T(8,128)}, f32[768,512]{1,0:T(8,128)}, f32[768,128]{1,0:T(8,128)}) custom-call(s32[4]{0:T(128)S(1)} %slice.84.refs_0_, bf16[2,768,384]{2,1,0:T(8,128)(2,1)} %collective-permute-done.15.refs_1_, bf16[2,768,384]{2,1,0:T(8,128)(2,1)S(1)} %collective-permute-done.16.refs_2_, bf16[16,384,512]{2,1,0:T(8,128)(2,1)} %bitcast.59, ...), custom_call_target="tpu_custom_call" | custom-call | flops 2415919104 | bytes 5505024 | tf_op jit(solution)/shard_map/pallas_call | solution.py:297
  133.6 4.7 %collective-permute-done.18.refs_2_ = bf16[2,768,384]{2,1,0:T(8,128)(2,1)} collective-permute-done((bf16[2,768,384]{2,1,0:T(8,128)(2,1)S(1)}, bf16[2,768,384]{2,1,0:T(8,128)(2,1)}, u32[]{:S(2)}, u32[]{:S(2)}) %collective-permute-start.18) | collective-permute-done | bytes 1179680 | tf_op jit(solution)/shard_map/ppermute | solution.py:32
  138.3 10.5 %shard_map.158 = (bf16[768,512]{1,0:T(8,128)(2,1)S(1)}, bf16[96,3072]{1,0:T(8,128)(2,1)}, bf16[96,3072]{1,0:T(8,128)(2,1)}, bf16[192,3072]{1,0:T(8,128)(2,1)}, b...) custom-call(s32[4]{0:T(128)S(1)} %slice.80.refs_0_, bf16[2,768,384]{2,1,0:T(8,128)(2,1)S(1)} %collective-permute-done.14.refs_1_, ...), custom_call_target="tpu_custom_call" | custom-call | flops 2415919104 | bytes 5505024 | tf_op jit(solution)/shard_map/pallas_call | solution.py:297
  149.1 2.7 %collective-permute-start.20 = (bf16[96,3072]{1,0:T(8,128)(2,1)}, bf16[96,3072]{1,0:T(8,128)(2,1)S(1)}, u32[]{:S(2)}, u32[]{:S(2)}) collective-permute-start(bf16[96,3072]{1,0:T(8,128)(2,1)} %get-tuple-element.62), channel_id=1, source_target_pairs={{0,12},{1,13},{2,14},{3,15},{4,0},{5,1},{6,2},{7,3},{8,4},{9,5},{1... | collective-permute-start | bytes 1769480 | tf_op jit(solution)/shard_map/ppermute | solution.py:32
  151.8 5.9 %shard_map.159 = (bf16[96,3072]{1,0:T(8,128)(2,1)}, bf16[96,3072]{1,0:T(8,128)(2,1)}, bf16[192,3072]{1,0:T(8,128)(2,1)}, bf16[192,3072]{1,0:T(8,128)(2,1)}, bf16[192,3072]{1,0:T(8,128)(2,1)}) custom-call(bf16[768,512]{1,0:T(8,128)(2,1)S(1)} %get-tuple-element.58.refs_0_, bf16[512,6144]{1,0:T(8,128)(2,1)} %bitcast.65), custom_call_target="tpu_custom_call" | custom-call | flops 2415919104 | bytes 8388608 | tf_op jit(solution)/shard_map/pallas_call | solution.py:323
  159.6 2.7 %collective-permute-start.25 = (bf16[96,3072]{1,0:T(8,128)(2,1)}, bf16[96,3072]{1,0:T(8,128)(2,1)S(1)}, u32[]{:S(2)}, u32[]{:S(2)}) collective-permute-start(bf16[96,3072]{1,0:T(8,128)(2,1)} %get-tuple-element.70), channel_id=1, source_target_pairs={{0,12},{1,13},{2,14},{3,15},{4,0},{5,1},{6,2},{7,3},{8,4},{9,5},{1... | collective-permute-start | bytes 1769480 | tf_op jit(solution)/shard_map/ppermute | solution.py:32
  163.0 2.7 %collective-permute-start.22 = (bf16[192,3072]{1,0:T(8,128)(2,1)S(1)}, bf16[192,3072]{1,0:T(8,128)(2,1)S(1)}, u32[]{:S(2)}, u32[]{:S(2)}) collective-permute-start(bf16[192,3072]{1,0:T(8,128)(2,1)S(1)} %fusion.6), channel_id=1, source_target_pairs={{0,12},{1,13},{2,14},{3,15},{4,0},{5,1},{6,2},{7,3},{8,4},{9,5},{1... | collective-permute-start | bytes 3538952 | tf_op jit(solution)/shard_map/ppermute | solution.py:32
  165.7 4.3 %collective-permute-done.23 = bf16[96,3072]{1,0:T(8,128)(2,1)S(1)} collective-permute-done((bf16[96,3072]{1,0:T(8,128)(2,1)}, bf16[96,3072]{1,0:T(8,128)(2,1)S(1)}, u32[]{:S(2)}, u32[]{:S(2)}) %collective-permute-start.23) | collective-permute-done | bytes 589856 | tf_op jit(solution)/shard_map/ppermute | solution.py:32
  170.8 2.7 %collective-permute-start.26 = (bf16[192,3072]{1,0:T(8,128)(2,1)S(1)}, bf16[192,3072]{1,0:T(8,128)(2,1)S(1)}, u32[]{:S(2)}, u32[]{:S(2)}) collective-permute-start(bf16[192,3072]{1,0:T(8,128)(2,1)S(1)} %fusion.8), channel_id=1, source_target_pairs={{0,12},{1,13},{2,14},{3,15},{4,0},{5,1},{6,2},{7,3},{8,4},{9,5},{1... | collective-permute-start | bytes 3538952 | tf_op jit(solution)/shard_map/ppermute | solution.py:32
  173.5 9.2 %collective-permute-done.21 = bf16[192,3072]{1,0:T(8,128)(2,1)S(1)} collective-permute-done((bf16[192,3072]{1,0:T(8,128)(2,1)S(1)}, bf16[192,3072]{1,0:T(8,128)(2,1)S(1)}, u32[]{:S(2)}, u32[]{:S(2)}) %collective-permute-start.21) | collective-permute-done | bytes 1179680 | tf_op jit(solution)/shard_map/ppermute | solution.py:32
  183.2 12.0 %collective-permute-done.24 = bf16[192,3072]{1,0:T(8,128)(2,1)S(1)} collective-permute-done((bf16[192,3072]{1,0:T(8,128)(2,1)S(1)}, bf16[192,3072]{1,0:T(8,128)(2,1)S(1)}, u32[]{:S(2)}, u32[]{:S(2)}) %collective-permute-start.24) | collective-permute-done | bytes 1179680 | tf_op jit(solution)/shard_map/ppermute | solution.py:32
  198.3 2.6 %collective-permute-start.28 = (bf16[48,6144]{1,0:T(8,128)(2,1)}, bf16[48,6144]{1,0:T(8,128)(2,1)}, u32[]{:S(2)}, u32[]{:S(2)}) collective-permute-start(bf16[48,6144]{1,0:T(8,128)(2,1)} %get-tuple-element.81), channel_id=1, source_target_pairs={{0,1},{1,2},{2,3},{3,0},{4,5},{5,6},{6,7},{7,4},{8,9},{9,10},{10,1... | collective-permute-start | bytes 1769480 | tf_op jit(solution)/shard_map/ppermute | solution.py:32
  201.0 7.0 %collective-permute-done.27 = bf16[48,6144]{1,0:T(8,128)(2,1)} collective-permute-done((bf16[48,6144]{1,0:T(8,128)(2,1)}, bf16[48,6144]{1,0:T(8,128)(2,1)}, u32[]{:S(2)}, u32[]{:S(2)}) %collective-permute-start.27) | collective-permute-done | bytes 589856 | tf_op jit(solution)/shard_map/ppermute | solution.py:32
  208.0 6.3 %collective-permute-done.28 = bf16[48,6144]{1,0:T(8,128)(2,1)} collective-permute-done((bf16[48,6144]{1,0:T(8,128)(2,1)}, bf16[48,6144]{1,0:T(8,128)(2,1)}, u32[]{:S(2)}, u32[]{:S(2)}) %collective-permute-start.28) | collective-permute-done | bytes 589856 | tf_op jit(solution)/shard_map/ppermute | solution.py:32
  218.0 9.1 %all-to-all-start.4 = ((bf16[8,6,6144]{2,1,0:T(8,128)(2,1)}), bf16[8,6,6144]{2,1,0:T(8,128)(2,1)S(1)}, u32[]{:S(2)}, u32[]{:S(2)}) async-start(bf16[8,6,6144]{2,1,0:T(8,128)(2,1)} %reshape.174), calls=%async_computation.4 | async-start | bytes 1572864 | tf_op jit(solution)/shard_map/all_to_all | solution.py:524
  227.3 12.0 %all-to-all-done.4 = bf16[8,6,6144]{2,1,0:T(8,128)(2,1)S(1)} async-done(((bf16[8,6,6144]{2,1,0:T(8,128)(2,1)}), bf16[8,6,6144]{2,1,0:T(8,128)(2,1)S(1)}, u32[]{:S(2)}, u32[]{:S(2)}) %all-to-all-start.4) | async-done | bytes 589856 | tf_op jit(solution)/shard_map/all_to_all | solution.py:524
  (147 shorter events, 47.9 us)
Async XLA Ops:
  6.5 40.7 %all-gather.3.cloned.1.call-start = ((), (), s32[]{:S(2)}) async-start(), calls=%async_computation.5 | async-start | bytes 5308416 | tf_op jit(solution)/shard_map/all_gather | solution.py:441
  10.8 11.7 %all-to-all-start = ((bf16[8,16,768]{2,1,0:T(8,128)(2,1)}), bf16[8,16,768]{2,1,0:T(8,128)(2,1)S(1)}, u32[]{:S(2)}, u32[]{:S(2)}) async-start(bf16[8,16,768]{2,1,0:T(8,128)(2,1)} %bitcast.6), calls=%async_computation | async-start | bytes 393216 | tf_op jit(solution)/shard_map/all_to_all | solution.py:444
  22.5 11.5 %collective-permute-start = (bf16[8,16,768]{2,1,0:T(8,128)(2,1)S(1)}, bf16[8,16,768]{2,1,0:T(8,128)(2,1)S(1)}, u32[]{:S(2)}, u32[]{:S(2)}) collective-permute-start(bf16[8,16,768]{2,1,0:T(8,128)(2,1)S(1)} %all-to-all-done), channel_id=1, source_target_pairs={{0,4},{1,5},{2,6},{3,7},{4,8},{5,9},{6,10},{7,11},{8,12},{9,13},{1... | collective-permute-start | bytes 589832 | tf_op jit(solution)/shard_map/ppermute | solution.py:32
  24.0 11.4 %collective-permute-start.2 = (bf16[8,16,768]{2,1,0:T(8,128)(2,1)S(1)}, bf16[8,16,768]{2,1,0:T(8,128)(2,1)S(1)}, u32[]{:S(2)}, u32[]{:S(2)}) collective-permute-start(bf16[8,16,768]{2,1,0:T(8,128)(2,1)S(1)} %all-to-all-done), channel_id=1, source_target_pairs={{0,8},{1,9},{2,10},{3,11},{4,12},{5,13},{6,14},{7,15},{8,0},{9,1},... | collective-permute-start | bytes 589832 | tf_op jit(solution)/shard_map/ppermute | solution.py:32
  26.7 8.7 %collective-permute-start.1 = (bf16[8,16,768]{2,1,0:T(8,128)(2,1)S(1)}, bf16[8,16,768]{2,1,0:T(8,128)(2,1)S(1)}, u32[]{:S(2)}, u32[]{:S(2)}) collective-permute-start(bf16[8,16,768]{2,1,0:T(8,128)(2,1)S(1)} %all-to-all-done), channel_id=1, source_target_pairs={{0,12},{1,13},{2,14},{3,15},{4,0},{5,1},{6,2},{7,3},{8,4},{9,5},{1... | collective-permute-start | bytes 589832 | tf_op jit(solution)/shard_map/ppermute | solution.py:32
  28.5 19.7 %all-to-all-start.1 = ((bf16[16,16,512]{2,1,0:T(8,128)(2,1)}), bf16[16,16,512]{2,1,0:T(8,128)(2,1)S(1)}, u32[]{:S(2)}, u32[]{:S(2)}) async-start(bf16[16,16,512]{2,1,0:T(8,128)(2,1)} %pad_maximum_fusion.5), calls=%async_computation.1 | async-start | bytes 524288 | tf_op jit(solution)/shard_map/all_to_all | solution.py:463
  34.0 13.2 %collective-permute-start.3 = (bf16[2,8,16,768]{3,2,1,0:T(8,128)(2,1)S(1)}, bf16[2,8,16,768]{3,2,1,0:T(8,128)(2,1)S(1)}, u32[]{:S(2)}, u32[]{:S(2)}) collective-permute-start(bf16[2,8,16,768]{3,2,1,0:T(8,128)(2,1)S(1)} %pad_maximum_fusion.3.refs_0_), channel_id=1, source_target_pairs={{0,1},{1,2},{2,3},{3,0},{4,5},{5,6},{6,7},{7,4},{8,9},{9,10},{10,1... | collective-permute-start | bytes 1179656 | tf_op jit(solution)/shard_map/ppermute | solution.py:32
  35.5 9.6 %collective-permute-start.6 = (bf16[2,8,16,768]{3,2,1,0:T(8,128)(2,1)S(1)}, bf16[2,8,16,768]{3,2,1,0:T(8,128)(2,1)S(1)}, u32[]{:S(2)}, u32[]{:S(2)}) collective-permute-start(bf16[2,8,16,768]{3,2,1,0:T(8,128)(2,1)S(1)} %pad_maximum_fusion.4.refs_1_), channel_id=1, source_target_pairs={{0,3},{1,0},{2,1},{3,2},{4,7},{5,4},{6,5},{7,6},{8,11},{9,8},{10,9... | collective-permute-start | bytes 1179656 | tf_op jit(solution)/shard_map/ppermute | solution.py:32
  38.0 11.2 %collective-permute-start.5 = (bf16[2,8,16,768]{3,2,1,0:T(8,128)(2,1)S(1)}, bf16[2,8,16,768]{3,2,1,0:T(8,128)(2,1)S(1)}, u32[]{:S(2)}, u32[]{:S(2)}) collective-permute-start(bf16[2,8,16,768]{3,2,1,0:T(8,128)(2,1)S(1)} %pad_maximum_fusion.4.refs_1_), channel_id=1, source_target_pairs={{0,1},{1,2},{2,3},{3,0},{4,5},{5,6},{6,7},{7,4},{8,9},{9,10},{10,1... | collective-permute-start | bytes 1179656 | tf_op jit(solution)/shard_map/ppermute | solution.py:32
  38.2 11.0 %collective-permute-start.4 = (bf16[2,8,16,768]{3,2,1,0:T(8,128)(2,1)S(1)}, bf16[2,8,16,768]{3,2,1,0:T(8,128)(2,1)S(1)}, u32[]{:S(2)}, u32[]{:S(2)}) collective-permute-start(bf16[2,8,16,768]{3,2,1,0:T(8,128)(2,1)S(1)} %pad_maximum_fusion.3.refs_0_), channel_id=1, source_target_pairs={{0,3},{1,0},{2,1},{3,2},{4,7},{5,4},{6,5},{7,6},{8,11},{9,8},{10,9... | collective-permute-start | bytes 1179656 | tf_op jit(solution)/shard_map/ppermute | solution.py:32
  75.5 10.2 %collective-permute-start.9 = (bf16[768,384]{1,0:T(8,128)(2,1)S(1)}, bf16[768,384]{1,0:T(8,128)(2,1)S(1)}, u32[]{:S(2)}, u32[]{:S(2)}) collective-permute-start(bf16[768,384]{1,0:T(8,128)(2,1)S(1)} %bitcast.66), channel_id=1, source_target_pairs={{0,4},{1,5},{2,6},{3,7},{4,8},{5,9},{6,10},{7,11},{8,12},{9,13},{1... | collective-permute-start | bytes 1769480 | tf_op jit(solution)/shard_map/ppermute | solution.py:32
  75.6 11.0 %collective-permute-start.11 = (bf16[768,384]{1,0:T(8,128)(2,1)S(1)}, bf16[768,384]{1,0:T(8,128)(2,1)S(1)}, u32[]{:S(2)}, u32[]{:S(2)}) collective-permute-start(bf16[768,384]{1,0:T(8,128)(2,1)S(1)} %bitcast.67), channel_id=1, source_target_pairs={{0,12},{1,13},{2,14},{3,15},{4,0},{5,1},{6,2},{7,3},{8,4},{9,5},{1... | collective-permute-start | bytes 1769480 | tf_op jit(solution)/shard_map/ppermute | solution.py:32
  78.2 16.0 %all-to-all-start.3 = ((bf16[16,16,384]{2,1,0:T(8,128)(2,1)}), bf16[16,16,384]{2,1,0:T(8,128)(2,1)S(1)}, u32[]{:S(2)}, u32[]{:S(2)}) async-start(bf16[16,16,384]{2,1,0:T(8,128)(2,1)} %copy-done.1), calls=%async_computation.3 | async-start | bytes 393216 | tf_op jit(solution)/shard_map/all_to_all | solution.py:480
  85.8 8.4 %collective-permute-start.10 = (bf16[384,384]{1,0:T(8,128)(2,1)S(1)}, bf16[384,384]{1,0:T(8,128)(2,1)S(1)}, u32[]{:S(2)}, u32[]{:S(2)}) collective-permute-start(bf16[384,384]{1,0:T(8,128)(2,1)S(1)} %slice.99), channel_id=1, source_target_pairs={{0,4},{1,5},{2,6},{3,7},{4,8},{5,9},{6,10},{7,11},{8,12},{9,13},{1... | collective-permute-start | bytes 884744 | tf_op jit(solution)/shard_map/ppermute | solution.py:32
  91.3 17.1 %collective-permute-start.13 = (bf16[2,768,384]{2,1,0:T(8,128)(2,1)}, bf16[2,768,384]{2,1,0:T(8,128)(2,1)}, u32[]{:S(2)}, u32[]{:S(2)}) collective-permute-start(bf16[2,768,384]{2,1,0:T(8,128)(2,1)} %pad_maximum_fusion.refs_1_), channel_id=1, source_target_pairs={{0,1},{1,2},{2,3},{3,0},{4,5},{5,6},{6,7},{7,4},{8,9},{9,10},{10,1... | collective-permute-start | bytes 3538952 | tf_op jit(solution)/shard_map/ppermute | solution.py:32
  93.0 16.2 %collective-permute-start.17 = (bf16[2,768,384]{2,1,0:T(8,128)(2,1)}, bf16[2,768,384]{2,1,0:T(8,128)(2,1)}, u32[]{:S(2)}, u32[]{:S(2)}) collective-permute-start(bf16[2,768,384]{2,1,0:T(8,128)(2,1)} %pad_maximum_fusion.refs_1_), channel_id=1, source_target_pairs={{0,3},{1,0},{2,1},{3,2},{4,7},{5,4},{6,5},{7,6},{8,11},{9,8},{10,9... | collective-permute-start | bytes 3538952 | tf_op jit(solution)/shard_map/ppermute | solution.py:32
  95.5 25.5 %collective-permute-start.15 = (bf16[2,768,384]{2,1,0:T(8,128)(2,1)}, bf16[2,768,384]{2,1,0:T(8,128)(2,1)}, u32[]{:S(2)}, u32[]{:S(2)}) collective-permute-start(bf16[2,768,384]{2,1,0:T(8,128)(2,1)} %pad_maximum_fusion.1.refs_2_), channel_id=1, source_target_pairs={{0,1},{1,2},{2,3},{3,0},{4,5},{5,6},{6,7},{7,4},{8,9},{9,10},{10,1... | collective-permute-start | bytes 3538952 | tf_op jit(solution)/shard_map/ppermute | solution.py:32
  96.7 25.1 %collective-permute-start.16 = (bf16[2,768,384]{2,1,0:T(8,128)(2,1)}, bf16[2,768,384]{2,1,0:T(8,128)(2,1)S(1)}, u32[]{:S(2)}, u32[]{:S(2)}) collective-permute-start(bf16[2,768,384]{2,1,0:T(8,128)(2,1)} %pad_maximum_fusion.1.refs_2_), channel_id=1, source_target_pairs={{0,3},{1,0},{2,1},{3,2},{4,7},{5,4},{6,5},{7,6},{8,11},{9,8},{10,9... | collective-permute-start | bytes 3538952 | tf_op jit(solution)/shard_map/ppermute | solution.py:32
  108.4 25.2 %collective-permute-start.14 = (bf16[2,768,384]{2,1,0:T(8,128)(2,1)}, bf16[2,768,384]{2,1,0:T(8,128)(2,1)S(1)}, u32[]{:S(2)}, u32[]{:S(2)}) collective-permute-start(bf16[2,768,384]{2,1,0:T(8,128)(2,1)} %collective-permute-done.13.refs_3_), channel_id=1, source_target_pairs={{0,1},{1,2},{2,3},{3,0},{4,5},{5,6},{6,7},{7,4},{8,9},{9,10},{10,1... | collective-permute-start | bytes 3538952 | tf_op jit(solution)/shard_map/ppermute | solution.py:32
  121.8 16.5 %collective-permute-start.18 = (bf16[2,768,384]{2,1,0:T(8,128)(2,1)S(1)}, bf16[2,768,384]{2,1,0:T(8,128)(2,1)}, u32[]{:S(2)}, u32[]{:S(2)}) collective-permute-start(bf16[2,768,384]{2,1,0:T(8,128)(2,1)S(1)} %collective-permute-done.16.refs_2_), channel_id=1, source_target_pairs={{0,3},{1,0},{2,1},{3,2},{4,7},{5,4},{6,5},{7,6},{8,11},{9,8},{10,9... | collective-permute-start | bytes 3538952 | tf_op jit(solution)/shard_map/ppermute | solution.py:32
  148.8 10.7 %collective-permute-start.19 = (bf16[96,3072]{1,0:T(8,128)(2,1)}, bf16[96,3072]{1,0:T(8,128)(2,1)S(1)}, u32[]{:S(2)}, u32[]{:S(2)}) collective-permute-start(bf16[96,3072]{1,0:T(8,128)(2,1)} %get-tuple-element.61), channel_id=1, source_target_pairs={{0,4},{1,5},{2,6},{3,7},{4,8},{5,9},{6,10},{7,11},{8,12},{9,13},{1... | collective-permute-start | bytes 1769480 | tf_op jit(solution)/shard_map/ppermute | solution.py:32
  149.1 10.4 %collective-permute-start.20 = (bf16[96,3072]{1,0:T(8,128)(2,1)}, bf16[96,3072]{1,0:T(8,128)(2,1)S(1)}, u32[]{:S(2)}, u32[]{:S(2)}) collective-permute-start(bf16[96,3072]{1,0:T(8,128)(2,1)} %get-tuple-element.62), channel_id=1, source_target_pairs={{0,12},{1,13},{2,14},{3,15},{4,0},{5,1},{6,2},{7,3},{8,4},{9,5},{1... | collective-permute-start | bytes 1769480 | tf_op jit(solution)/shard_map/ppermute | solution.py:32
  159.6 10.5 %collective-permute-start.23 = (bf16[96,3072]{1,0:T(8,128)(2,1)}, bf16[96,3072]{1,0:T(8,128)(2,1)S(1)}, u32[]{:S(2)}, u32[]{:S(2)}) collective-permute-start(bf16[96,3072]{1,0:T(8,128)(2,1)} %get-tuple-element.68), channel_id=1, source_target_pairs={{0,4},{1,5},{2,6},{3,7},{4,8},{5,9},{6,10},{7,11},{8,12},{9,13},{1... | collective-permute-start | bytes 1769480 | tf_op jit(solution)/shard_map/ppermute | solution.py:32
  159.6 10.9 %collective-permute-start.25 = (bf16[96,3072]{1,0:T(8,128)(2,1)}, bf16[96,3072]{1,0:T(8,128)(2,1)S(1)}, u32[]{:S(2)}, u32[]{:S(2)}) collective-permute-start(bf16[96,3072]{1,0:T(8,128)(2,1)} %get-tuple-element.70), channel_id=1, source_target_pairs={{0,12},{1,13},{2,14},{3,15},{4,0},{5,1},{6,2},{7,3},{8,4},{9,5},{1... | collective-permute-start | bytes 1769480 | tf_op jit(solution)/shard_map/ppermute | solution.py:32
  162.6 20.1 %collective-permute-start.21 = (bf16[192,3072]{1,0:T(8,128)(2,1)S(1)}, bf16[192,3072]{1,0:T(8,128)(2,1)S(1)}, u32[]{:S(2)}, u32[]{:S(2)}) collective-permute-start(bf16[192,3072]{1,0:T(8,128)(2,1)S(1)} %fusion.5), channel_id=1, source_target_pairs={{0,4},{1,5},{2,6},{3,7},{4,8},{5,9},{6,10},{7,11},{8,12},{9,13},{1... | collective-permute-start | bytes 3538952 | tf_op jit(solution)/shard_map/ppermute | solution.py:32
  163.0 19.7 %collective-permute-start.22 = (bf16[192,3072]{1,0:T(8,128)(2,1)S(1)}, bf16[192,3072]{1,0:T(8,128)(2,1)S(1)}, u32[]{:S(2)}, u32[]{:S(2)}) collective-permute-start(bf16[192,3072]{1,0:T(8,128)(2,1)S(1)} %fusion.6), channel_id=1, source_target_pairs={{0,12},{1,13},{2,14},{3,15},{4,0},{5,1},{6,2},{7,3},{8,4},{9,5},{1... | collective-permute-start | bytes 3538952 | tf_op jit(solution)/shard_map/ppermute | solution.py:32
  170.3 24.9 %collective-permute-start.24 = (bf16[192,3072]{1,0:T(8,128)(2,1)S(1)}, bf16[192,3072]{1,0:T(8,128)(2,1)S(1)}, u32[]{:S(2)}, u32[]{:S(2)}) collective-permute-start(bf16[192,3072]{1,0:T(8,128)(2,1)S(1)} %fusion.7), channel_id=1, source_target_pairs={{0,4},{1,5},{2,6},{3,7},{4,8},{5,9},{6,10},{7,11},{8,12},{9,13},{1... | collective-permute-start | bytes 3538952 | tf_op jit(solution)/shard_map/ppermute | solution.py:32
  170.8 24.5 %collective-permute-start.26 = (bf16[192,3072]{1,0:T(8,128)(2,1)S(1)}, bf16[192,3072]{1,0:T(8,128)(2,1)S(1)}, u32[]{:S(2)}, u32[]{:S(2)}) collective-permute-start(bf16[192,3072]{1,0:T(8,128)(2,1)S(1)} %fusion.8), channel_id=1, source_target_pairs={{0,12},{1,13},{2,14},{3,15},{4,0},{5,1},{6,2},{7,3},{8,4},{9,5},{1... | collective-permute-start | bytes 3538952 | tf_op jit(solution)/shard_map/ppermute | solution.py:32
  197.1 10.9 %collective-permute-start.27 = (bf16[48,6144]{1,0:T(8,128)(2,1)}, bf16[48,6144]{1,0:T(8,128)(2,1)}, u32[]{:S(2)}, u32[]{:S(2)}) collective-permute-start(bf16[48,6144]{1,0:T(8,128)(2,1)} %get-tuple-element.79), channel_id=1, source_target_pairs={{0,2},{1,3},{2,0},{3,1},{4,6},{5,7},{6,4},{7,5},{8,10},{9,11},{10,... | collective-permute-start | bytes 1769480 | tf_op jit(solution)/shard_map/ppermute | solution.py:32
  198.3 16.0 %collective-permute-start.28 = (bf16[48,6144]{1,0:T(8,128)(2,1)}, bf16[48,6144]{1,0:T(8,128)(2,1)}, u32[]{:S(2)}, u32[]{:S(2)}) collective-permute-start(bf16[48,6144]{1,0:T(8,128)(2,1)} %get-tuple-element.81), channel_id=1, source_target_pairs={{0,1},{1,2},{2,3},{3,0},{4,5},{5,6},{6,7},{7,4},{8,9},{9,10},{10,1... | collective-permute-start | bytes 1769480 | tf_op jit(solution)/shard_map/ppermute | solution.py:32
  200.9 14.2 %collective-permute-start.29 = (bf16[48,6144]{1,0:T(8,128)(2,1)S(1)}, bf16[48,6144]{1,0:T(8,128)(2,1)}, u32[]{:S(2)}, u32[]{:S(2)}) collective-permute-start(bf16[48,6144]{1,0:T(8,128)(2,1)S(1)} %get-tuple-element.80), channel_id=1, source_target_pairs={{0,3},{1,0},{2,1},{3,2},{4,7},{5,4},{6,5},{7,6},{8,11},{9,8},{10,9... | collective-permute-start | bytes 1769480 | tf_op jit(solution)/shard_map/ppermute | solution.py:32
  218.0 21.4 %all-to-all-start.4 = ((bf16[8,6,6144]{2,1,0:T(8,128)(2,1)}), bf16[8,6,6144]{2,1,0:T(8,128)(2,1)S(1)}, u32[]{:S(2)}, u32[]{:S(2)}) async-start(bf16[8,6,6144]{2,1,0:T(8,128)(2,1)} %reshape.174), calls=%async_computation.4 | async-start | bytes 1572864 | tf_op jit(solution)/shard_map/all_to_all | solution.py:524
  (23 other events, 208.8 us)
Sparse Core Ops, SparseCore 0:
  9.0 37.8 all-gather.2

commit v2 on v1

--- a/solution.py
+++ b/solution.py
@@ -169,9 +169,10 @@
         sums_out, refs = refs[:3], refs[3:]
         gate_sum, up_sum, square_sum = refs[:3]
         refs = refs[3:]
-    held, weights, sems = refs[:count], refs[count : count + 2 * len(steps)], refs[-1]
-    carried = refs[count + 2 * len(steps) : -1]
-
+    held, weights, sems = refs[:count], refs[count : count + len(steps)], refs[-1]
+    carried = refs[count + len(steps) : -1]
+
+    hidden_width = gate.shape[2]
     copies, at, place, sem = [], 0, 0, 0
     for step, (shapes, column) in enumerate(steps):
         mine = []
@@ -180,11 +181,13 @@
             at, sem = at + 1, sem + 1
         width = shapes[0][2]
         for index in range(sum(shape[0] for shape in shapes)):
-            for source, target in ((gate, weights[2 * step]), (up, weights[2 * step + 1])):
+            for part, source in enumerate((gate, up)):
                 mine.append(
                     pltpu.make_async_copy(
                         source.at[order[place], pl.ds(column, width)],
-                        target.at[pl.ds(index * width, width)],
+                        weights[step].at[
+                            pl.ds(index * width, width), pl.ds(part * hidden_width, hidden_width)
+                        ],
                         sems.at[sem],
                     )
                 )
@@ -212,9 +215,9 @@
                 pieces.append(held[at][index])
             at += 1
         block = jnp.concatenate(pieces, axis=1)
-        gate_term = jnp.dot(block, weights[2 * step][...], preferred_element_type=F32)
+        both = jnp.dot(block, weights[step][...], preferred_element_type=F32)
+        gate_term, up_term = both[:, :hidden_width], both[:, hidden_width:]
         gate_sum[...] = gate_sum[...] + gate_term if step > 0 else gate_term
-        up_term = jnp.dot(block, weights[2 * step + 1][...], preferred_element_type=F32)
         up_sum[...] = up_sum[...] + up_term if step > 0 else up_term
         for piece in pieces:
             inverse = inverse_gain[order[place]][:, column : column + width]
@@ -287,7 +290,7 @@
     depth, copies = 0, len(blocks)
     for group, _ in steps:
         places = sum(block.shape[0] for block in group)
-        scratch += [pltpu.VMEM((places * group[0].shape[2], hidden), BF)] * 2
+        scratch.append(pltpu.VMEM((places * group[0].shape[2], 2 * hidden), BF))
         depth += places * group[0].shape[2]
         copies += 2 * places
     if begun:

time: 248 us -> 248 us (level)
  no operation moved by 1% of the time
where the time goes in v2:
time: 248 us; the launch traced here: 247 us
  waiting for transfers between devices  93 us (38%)
  starting transfers between devices  69.1 us (28%)
  Pallas kernels  38.5 us (16%)
  blocking collectives  15.1 us (6%)
  between operations  13.9 us (6%)
  other arithmetic  9.82 us (4%)
  local copies, waits for them, and re-layouts  6.61 us (3%)
    ppermute x30, waiting for transfers between devices, send(): return lax.ppermute(block, ('head', 'expert'), ring_pairs(near, step))  75.5 us
    ppermute x30, starting transfers between devices, send(): return lax.ppermute(block, ('head', 'expert'), ring_pairs(near, step))  44.3 us
    pallas_call x3, Pallas kernels, gate_up(): pl.pallas_call(lambda *refs: gate_up_kernel(shapes, finish, begun, len(pr...  26.9 us
    all_to_all x1, blocking collectives, per_device(): lax.all_to_all(slots, 'head', split_axis=0, concat_axis=0, tiled=True)  15.1 us
    all_to_all x1, waiting for transfers between devices, per_device(): lax.all_to_all(totals, 'head', split_axis=0, concat_axis=0, tiled=True)  12 us
    all_to_all x1, starting transfers between devices, per_device(): lax.all_to_all(totals, 'head', split_axis=0, concat_axis=0, tiled=True)  9.1 us
    pallas_call x1, Pallas kernels, down(): pl.pallas_call(lambda *refs: down_kernel(start, *refs), out_shape=[pltpu....  5.95 us
    all_to_all x1, starting transfers between devices, per_device(): lax.all_to_all(merged, 'head', split_axis=0, concat_axis=0, tiled=True)  5.81 us
  transfers between devices with their start and end apart: 35, of which 21 were waited for; matrix products, arithmetic and copies ran while one was open for 4% of the time, Pallas kernels for 10%

profile of v2, /device:TPU:1, one launch (start us, length us, event | category | flops | bytes accessed | tf_op | source)
XLA Modules:
  0.0 247.5 jit_solution(3345430714559892875)
XLA Ops:
  7.9 2.9 %shard_map.154 = bf16[128,768]{1,0:T(8,128)(2,1)} custom-call(s32[1]{0:T(128)} %bitcast.1.first_head, s32[1,8]{1,0:T(1,128)S(1)} %copy-done.2, bf16[128,768]{1,0:T(8,128)(2,1)} %bitcast.77, bf16[128,128]{1,0:T(8,128)(2,1)} %bitcast.82, bf16[128,128]{1,0:T(8,128)(2,1)} %bitcast.83, bf16[128,768]{1,0:T(8,128)(2,1)} %bitcast.78), custom_call_target="tpu_custom_call" | custom-call | flops 50331648 | bytes 1048576 | tf_op jit(solution)/shard_map/pallas_call | solution.py:399
  10.8 5.8 %all-to-all-start = ((bf16[8,16,768]{2,1,0:T(8,128)(2,1)}), bf16[8,16,768]{2,1,0:T(8,128)(2,1)S(1)}, u32[]{:S(2)}, u32[]{:S(2)}) async-start(bf16[8,16,768]{2,1,0:T(8,128)(2,1)} %bitcast.6), calls=%async_computation | async-start | bytes 393216 | tf_op jit(solution)/shard_map/all_to_all | solution.py:447
  17.7 4.8 %all-to-all-done = bf16[8,16,768]{2,1,0:T(8,128)(2,1)S(1)} async-done(((bf16[8,16,768]{2,1,0:T(8,128)(2,1)}), bf16[8,16,768]{2,1,0:T(8,128)(2,1)S(1)}, u32[]{:S(2)}, u32[]{:S(2)}) %all-to-all-start) | async-done | bytes 196640 | tf_op jit(solution)/shard_map/all_to_all | solution.py:447
  24.0 2.7 %collective-permute-start.2 = (bf16[8,16,768]{2,1,0:T(8,128)(2,1)S(1)}, bf16[8,16,768]{2,1,0:T(8,128)(2,1)S(1)}, u32[]{:S(2)}, u32[]{:S(2)}) collective-permute-start(bf16[8,16,768]{2,1,0:T(8,128)(2,1)S(1)} %all-to-all-done), channel_id=1, source_target_pairs={{0,8},{1,9},{2,10},{3,11},{4,12},{5,13},{6,14},{7,15},{8,0},{9,1},... | collective-permute-start | bytes 589832 | tf_op jit(solution)/shard_map/ppermute | solution.py:32
  28.5 5.4 %all-to-all-start.1 = ((bf16[16,16,512]{2,1,0:T(8,128)(2,1)}), bf16[16,16,512]{2,1,0:T(8,128)(2,1)S(1)}, u32[]{:S(2)}, u32[]{:S(2)}) async-start(bf16[16,16,512]{2,1,0:T(8,128)(2,1)} %pad_maximum_fusion.5), calls=%async_computation.1 | async-start | bytes 524288 | tf_op jit(solution)/shard_map/all_to_all | solution.py:466
  40.7 4.3 %collective-permute-done.6.refs_5_ = bf16[2,8,16,768]{3,2,1,0:T(8,128)(2,1)S(1)} collective-permute-done((bf16[2,8,16,768]{3,2,1,0:T(8,128)(2,1)S(1)}, bf16[2,8,16,768]{3,2,1,0:T(8,128)(2,1)S(1)}, u32[]{:S(2)}, u32[]{:S(2)}) %collective-permute-start.6) | collective-permute-done | bytes 393248 | tf_op jit(solution)/shard_map/ppermute | solution.py:32
  49.2 4.1 %collective-permute-done.8.refs_7_ = bf16[2,8,16,768]{3,2,1,0:T(8,128)(2,1)S(1)} collective-permute-done((bf16[2,8,16,768]{3,2,1,0:T(8,128)(2,1)S(1)}, bf16[2,8,16,768]{3,2,1,0:T(8,128)(2,1)S(1)}, u32[]{:S(2)}, u32[]{:S(2)}) %collective-permute-start.8) | collective-permute-done | bytes 393248 | tf_op jit(solution)/shard_map/ppermute | solution.py:32
  57.7 2.8 %shard_map.155 = (bf16[16,16,384]{2,1,0:T(8,128)(2,1)S(1)}, bf16[768,384]{1,0:T(8,128)(2,1)S(1)}) custom-call(s32[16]{0:T(128)S(1)} %select_reduce_fusion.place, bf16[2,8,16,768]{3,2,1,0:T(8,128)(2,1)S(1)} %pad_maximum_fusion.3.refs_0_, bf16[2,8,16,768]{3,2,1,0:T(8,128)(2,1)S(1)} %pad_maximum_fusion.4.refs_1_, ...), custom_call_target="tpu_custom_call" | custom-call | flops 1207959552 | bytes 10485760 | tf_op jit(solution)/shard_map/pallas_call | solution.py:94
  60.5 15.1 %all_to_all.25 = bf16[8,96,384]{2,1,0:T(8,128)(2,1)S(1)} all-to-all(bf16[8,96,384]{2,1,0:T(8,128)(2,1)S(1)} %bitcast.53), channel_id=1, replica_groups=mesh['head'=8,'expert'=16] {'head'}, dimensions={0} | all-to-all | bytes 1179648 | tf_op jit(solution)/shard_map/all_to_all | solution.py:486
  75.6 2.7 %collective-permute-start.11 = (bf16[768,384]{1,0:T(8,128)(2,1)S(1)}, bf16[768,384]{1,0:T(8,128)(2,1)S(1)}, u32[]{:S(2)}, u32[]{:S(2)}) collective-permute-start(bf16[768,384]{1,0:T(8,128)(2,1)S(1)} %bitcast.67), channel_id=1, source_target_pairs={{0,12},{1,13},{2,14},{3,15},{4,0},{5,1},{6,2},{7,3},{8,4},{9,5},{1... | collective-permute-start | bytes 1769480 | tf_op jit(solution)/shard_map/ppermute | solution.py:32
  78.2 4.5 %all-to-all-start.3 = ((bf16[16,16,384]{2,1,0:T(8,128)(2,1)}), bf16[16,16,384]{2,1,0:T(8,128)(2,1)S(1)}, u32[]{:S(2)}, u32[]{:S(2)}) async-start(bf16[16,16,384]{2,1,0:T(8,128)(2,1)} %copy-done.1), calls=%async_computation.3 | async-start | bytes 393216 | tf_op jit(solution)/shard_map/all_to_all | solution.py:483
  82.7 3.0 %collective-permute-done.9 = bf16[768,384]{1,0:T(8,128)(2,1)S(1)} collective-permute-done((bf16[768,384]{1,0:T(8,128)(2,1)S(1)}, bf16[768,384]{1,0:T(8,128)(2,1)S(1)}, u32[]{:S(2)}, u32[]{:S(2)}) %collective-permute-start.9) | collective-permute-done | bytes 589856 | tf_op jit(solution)/shard_map/ppermute | solution.py:32
  86.5 3.5 %collective-permute-start.12 = (bf16[384,384]{1,0:T(8,128)(2,1)S(1)}, bf16[384,384]{1,0:T(8,128)(2,1)S(1)}, u32[]{:S(2)}, u32[]{:S(2)}) collective-permute-start(bf16[384,384]{1,0:T(8,128)(2,1)S(1)} %slice.100), channel_id=1, source_target_pairs={{0,12},{1,13},{2,14},{3,15},{4,0},{5,1},{6,2},{7,3},{8,4},{9,5},{1... | collective-permute-start | bytes 884744 | tf_op jit(solution)/shard_map/ppermute | solution.py:32
  98.3 10.1 %collective-permute-done.13.refs_3_ = bf16[2,768,384]{2,1,0:T(8,128)(2,1)} collective-permute-done((bf16[2,768,384]{2,1,0:T(8,128)(2,1)}, bf16[2,768,384]{2,1,0:T(8,128)(2,1)}, u32[]{:S(2)}, u32[]{:S(2)}) %collective-permute-start.13) | collective-permute-done | bytes 1179680 | tf_op jit(solution)/shard_map/ppermute | solution.py:32
  109.2 9.3 %shard_map.156 = (f32[768,512]{1,0:T(8,128)}, f32[768,512]{1,0:T(8,128)}, f32[768,128]{1,0:T(8,128)}) custom-call(s32[8]{0:T(128)S(1)} %slice.82.refs_0_, bf16[2,768,384]{2,1,0:T(8,128)(2,1)} %pad_maximum_fusion.refs_1_, bf16[2,768,384]{2,1,0:T(8,128)(2,1)} %pad_maximum_fusion.1.refs_2_, bf16[2,768,384]{2,1,0:T(8,128)(2,1)} %collective-permute-done.13.refs_3_, ...), custom_call_target="tpu_custom_call" | custom-call | flops 4831838208 | bytes 11010048 | tf_op jit(solution)/shard_map/pallas_call | solution.py:300
  121.8 3.3 %collective-permute-start.18 = (bf16[2,768,384]{2,1,0:T(8,128)(2,1)S(1)}, bf16[2,768,384]{2,1,0:T(8,128)(2,1)}, u32[]{:S(2)}, u32[]{:S(2)}) collective-permute-start(bf16[2,768,384]{2,1,0:T(8,128)(2,1)S(1)} %collective-permute-done.16.refs_2_), channel_id=1, source_target_pairs={{0,3},{1,0},{2,1},{3,2},{4,7},{5,4},{6,5},{7,6},{8,11},{9,8},{10,9... | collective-permute-start | bytes 3538952 | tf_op jit(solution)/shard_map/ppermute | solution.py:32
  125.7 7.0 %shard_map.157 = (f32[768,512]{1,0:T(8,128)}, f32[768,512]{1,0:T(8,128)}, f32[768,128]{1,0:T(8,128)}) custom-call(s32[4]{0:T(128)S(1)} %slice.84.refs_0_, bf16[2,768,384]{2,1,0:T(8,128)(2,1)} %collective-permute-done.15.refs_1_, bf16[2,768,384]{2,1,0:T(8,128)(2,1)S(1)} %collective-permute-done.16.refs_2_, bf16[16,384,512]{2,1,0:T(8,128)(2,1)} %bitcast.59, ...), custom_call_target="tpu_custom_call" | custom-call | flops 2415919104 | bytes 5505024 | tf_op jit(solution)/shard_map/pallas_call | solution.py:300
  133.6 4.7 %collective-permute-done.18.refs_2_ = bf16[2,768,384]{2,1,0:T(8,128)(2,1)} collective-permute-done((bf16[2,768,384]{2,1,0:T(8,128)(2,1)S(1)}, bf16[2,768,384]{2,1,0:T(8,128)(2,1)}, u32[]{:S(2)}, u32[]{:S(2)}) %collective-permute-start.18) | collective-permute-done | bytes 1179680 | tf_op jit(solution)/shard_map/ppermute | solution.py:32
  138.3 10.5 %shard_map.158 = (bf16[768,512]{1,0:T(8,128)(2,1)S(1)}, bf16[96,3072]{1,0:T(8,128)(2,1)}, bf16[96,3072]{1,0:T(8,128)(2,1)}, bf16[192,3072]{1,0:T(8,128)(2,1)}, b...) custom-call(s32[4]{0:T(128)S(1)} %slice.80.refs_0_, bf16[2,768,384]{2,1,0:T(8,128)(2,1)S(1)} %collective-permute-done.14.refs_1_, ...), custom_call_target="tpu_custom_call" | custom-call | flops 2415919104 | bytes 5505024 | tf_op jit(solution)/shard_map/pallas_call | solution.py:300
  148.9 2.7 %collective-permute-start.20 = (bf16[96,3072]{1,0:T(8,128)(2,1)}, bf16[96,3072]{1,0:T(8,128)(2,1)S(1)}, u32[]{:S(2)}, u32[]{:S(2)}) collective-permute-start(bf16[96,3072]{1,0:T(8,128)(2,1)} %get-tuple-element.62), channel_id=1, source_target_pairs={{0,12},{1,13},{2,14},{3,15},{4,0},{5,1},{6,2},{7,3},{8,4},{9,5},{1... | collective-permute-start | bytes 1769480 | tf_op jit(solution)/shard_map/ppermute | solution.py:32
  151.6 5.9 %shard_map.159 = (bf16[96,3072]{1,0:T(8,128)(2,1)}, bf16[96,3072]{1,0:T(8,128)(2,1)}, bf16[192,3072]{1,0:T(8,128)(2,1)}, bf16[192,3072]{1,0:T(8,128)(2,1)}, bf16[192,3072]{1,0:T(8,128)(2,1)}) custom-call(bf16[768,512]{1,0:T(8,128)(2,1)S(1)} %get-tuple-element.58.refs_0_, bf16[512,6144]{1,0:T(8,128)(2,1)} %bitcast.65), custom_call_target="tpu_custom_call" | custom-call | flops 2415919104 | bytes 8388608 | tf_op jit(solution)/shard_map/pallas_call | solution.py:326
  159.3 2.7 %collective-permute-start.25 = (bf16[96,3072]{1,0:T(8,128)(2,1)}, bf16[96,3072]{1,0:T(8,128)(2,1)S(1)}, u32[]{:S(2)}, u32[]{:S(2)}) collective-permute-start(bf16[96,3072]{1,0:T(8,128)(2,1)} %get-tuple-element.70), channel_id=1, source_target_pairs={{0,12},{1,13},{2,14},{3,15},{4,0},{5,1},{6,2},{7,3},{8,4},{9,5},{1... | collective-permute-start | bytes 1769480 | tf_op jit(solution)/shard_map/ppermute | solution.py:32
  162.8 2.9 %collective-permute-start.22 = (bf16[192,3072]{1,0:T(8,128)(2,1)S(1)}, bf16[192,3072]{1,0:T(8,128)(2,1)S(1)}, u32[]{:S(2)}, u32[]{:S(2)}) collective-permute-start(bf16[192,3072]{1,0:T(8,128)(2,1)S(1)} %fusion.6), channel_id=1, source_target_pairs={{0,12},{1,13},{2,14},{3,15},{4,0},{5,1},{6,2},{7,3},{8,4},{9,5},{1... | collective-permute-start | bytes 3538952 | tf_op jit(solution)/shard_map/ppermute | solution.py:32
  165.7 4.1 %collective-permute-done.23 = bf16[96,3072]{1,0:T(8,128)(2,1)S(1)} collective-permute-done((bf16[96,3072]{1,0:T(8,128)(2,1)}, bf16[96,3072]{1,0:T(8,128)(2,1)S(1)}, u32[]{:S(2)}, u32[]{:S(2)}) %collective-permute-start.23) | collective-permute-done | bytes 589856 | tf_op jit(solution)/shard_map/ppermute | solution.py:32
  170.5 2.7 %collective-permute-start.26 = (bf16[192,3072]{1,0:T(8,128)(2,1)S(1)}, bf16[192,3072]{1,0:T(8,128)(2,1)S(1)}, u32[]{:S(2)}, u32[]{:S(2)}) collective-permute-start(bf16[192,3072]{1,0:T(8,128)(2,1)S(1)} %fusion.8), channel_id=1, source_target_pairs={{0,12},{1,13},{2,14},{3,15},{4,0},{5,1},{6,2},{7,3},{8,4},{9,5},{1... | collective-permute-start | bytes 3538952 | tf_op jit(solution)/shard_map/ppermute | solution.py:32
  173.3 9.2 %collective-permute-done.21 = bf16[192,3072]{1,0:T(8,128)(2,1)S(1)} collective-permute-done((bf16[192,3072]{1,0:T(8,128)(2,1)S(1)}, bf16[192,3072]{1,0:T(8,128)(2,1)S(1)}, u32[]{:S(2)}, u32[]{:S(2)}) %collective-permute-start.21) | collective-permute-done | bytes 1179680 | tf_op jit(solution)/shard_map/ppermute | solution.py:32
  183.0 12.0 %collective-permute-done.24 = bf16[192,3072]{1,0:T(8,128)(2,1)S(1)} collective-permute-done((bf16[192,3072]{1,0:T(8,128)(2,1)S(1)}, bf16[192,3072]{1,0:T(8,128)(2,1)S(1)}, u32[]{:S(2)}, u32[]{:S(2)}) %collective-permute-start.24) | collective-permute-done | bytes 1179680 | tf_op jit(solution)/shard_map/ppermute | solution.py:32
  198.0 2.6 %collective-permute-start.28 = (bf16[48,6144]{1,0:T(8,128)(2,1)}, bf16[48,6144]{1,0:T(8,128)(2,1)}, u32[]{:S(2)}, u32[]{:S(2)}) collective-permute-start(bf16[48,6144]{1,0:T(8,128)(2,1)} %get-tuple-element.81), channel_id=1, source_target_pairs={{0,1},{1,2},{2,3},{3,0},{4,5},{5,6},{6,7},{7,4},{8,9},{9,10},{10,1... | collective-permute-start | bytes 1769480 | tf_op jit(solution)/shard_map/ppermute | solution.py:32
  200.8 7.0 %collective-permute-done.27 = bf16[48,6144]{1,0:T(8,128)(2,1)} collective-permute-done((bf16[48,6144]{1,0:T(8,128)(2,1)}, bf16[48,6144]{1,0:T(8,128)(2,1)}, u32[]{:S(2)}, u32[]{:S(2)}) %collective-permute-start.27) | collective-permute-done | bytes 589856 | tf_op jit(solution)/shard_map/ppermute | solution.py:32
  207.8 6.3 %collective-permute-done.28 = bf16[48,6144]{1,0:T(8,128)(2,1)} collective-permute-done((bf16[48,6144]{1,0:T(8,128)(2,1)}, bf16[48,6144]{1,0:T(8,128)(2,1)}, u32[]{:S(2)}, u32[]{:S(2)}) %collective-permute-start.28) | collective-permute-done | bytes 589856 | tf_op jit(solution)/shard_map/ppermute | solution.py:32
  217.8 9.1 %all-to-all-start.4 = ((bf16[8,6,6144]{2,1,0:T(8,128)(2,1)}), bf16[8,6,6144]{2,1,0:T(8,128)(2,1)S(1)}, u32[]{:S(2)}, u32[]{:S(2)}) async-start(bf16[8,6,6144]{2,1,0:T(8,128)(2,1)} %reshape.174), calls=%async_computation.4 | async-start | bytes 1572864 | tf_op jit(solution)/shard_map/all_to_all | solution.py:527
  227.1 12.0 %all-to-all-done.4 = bf16[8,6,6144]{2,1,0:T(8,128)(2,1)S(1)} async-done(((bf16[8,6,6144]{2,1,0:T(8,128)(2,1)}), bf16[8,6,6144]{2,1,0:T(8,128)(2,1)S(1)}, u32[]{:S(2)}, u32[]{:S(2)}) %all-to-all-start.4) | async-done | bytes 589856 | tf_op jit(solution)/shard_map/all_to_all | solution.py:527
  (147 shorter events, 47.7 us)
Async XLA Ops:
  6.5 40.7 %all-gather.3.cloned.1.call-start = ((), (), s32[]{:S(2)}) async-start(), calls=%async_computation.5 | async-start | bytes 5308416 | tf_op jit(solution)/shard_map/all_gather | solution.py:444
  10.8 11.7 %all-to-all-start = ((bf16[8,16,768]{2,1,0:T(8,128)(2,1)}), bf16[8,16,768]{2,1,0:T(8,128)(2,1)S(1)}, u32[]{:S(2)}, u32[]{:S(2)}) async-start(bf16[8,16,768]{2,1,0:T(8,128)(2,1)} %bitcast.6), calls=%async_computation | async-start | bytes 393216 | tf_op jit(solution)/shard_map/all_to_all | solution.py:447
  22.5 11.5 %collective-permute-start = (bf16[8,16,768]{2,1,0:T(8,128)(2,1)S(1)}, bf16[8,16,768]{2,1,0:T(8,128)(2,1)S(1)}, u32[]{:S(2)}, u32[]{:S(2)}) collective-permute-start(bf16[8,16,768]{2,1,0:T(8,128)(2,1)S(1)} %all-to-all-done), channel_id=1, source_target_pairs={{0,4},{1,5},{2,6},{3,7},{4,8},{5,9},{6,10},{7,11},{8,12},{9,13},{1... | collective-permute-start | bytes 589832 | tf_op jit(solution)/shard_map/ppermute | solution.py:32
  24.0 11.4 %collective-permute-start.2 = (bf16[8,16,768]{2,1,0:T(8,128)(2,1)S(1)}, bf16[8,16,768]{2,1,0:T(8,128)(2,1)S(1)}, u32[]{:S(2)}, u32[]{:S(2)}) collective-permute-start(bf16[8,16,768]{2,1,0:T(8,128)(2,1)S(1)} %all-to-all-done), channel_id=1, source_target_pairs={{0,8},{1,9},{2,10},{3,11},{4,12},{5,13},{6,14},{7,15},{8,0},{9,1},... | collective-permute-start | bytes 589832 | tf_op jit(solution)/shard_map/ppermute | solution.py:32
  26.7 8.7 %collective-permute-start.1 = (bf16[8,16,768]{2,1,0:T(8,128)(2,1)S(1)}, bf16[8,16,768]{2,1,0:T(8,128)(2,1)S(1)}, u32[]{:S(2)}, u32[]{:S(2)}) collective-permute-start(bf16[8,16,768]{2,1,0:T(8,128)(2,1)S(1)} %all-to-all-done), channel_id=1, source_target_pairs={{0,12},{1,13},{2,14},{3,15},{4,0},{5,1},{6,2},{7,3},{8,4},{9,5},{1... | collective-permute-start | bytes 589832 | tf_op jit(solution)/shard_map/ppermute | solution.py:32
  28.5 19.7 %all-to-all-start.1 = ((bf16[16,16,512]{2,1,0:T(8,128)(2,1)}), bf16[16,16,512]{2,1,0:T(8,128)(2,1)S(1)}, u32[]{:S(2)}, u32[]{:S(2)}) async-start(bf16[16,16,512]{2,1,0:T(8,128)(2,1)} %pad_maximum_fusion.5), calls=%async_computation.1 | async-start | bytes 524288 | tf_op jit(solution)/shard_map/all_to_all | solution.py:466
  34.0 13.2 %collective-permute-start.3 = (bf16[2,8,16,768]{3,2,1,0:T(8,128)(2,1)S(1)}, bf16[2,8,16,768]{3,2,1,0:T(8,128)(2,1)S(1)}, u32[]{:S(2)}, u32[]{:S(2)}) collective-permute-start(bf16[2,8,16,768]{3,2,1,0:T(8,128)(2,1)S(1)} %pad_maximum_fusion.3.refs_0_), channel_id=1, source_target_pairs={{0,1},{1,2},{2,3},{3,0},{4,5},{5,6},{6,7},{7,4},{8,9},{9,10},{10,1... | collective-permute-start | bytes 1179656 | tf_op jit(solution)/shard_map/ppermute | solution.py:32
  35.5 9.6 %collective-permute-start.6 = (bf16[2,8,16,768]{3,2,1,0:T(8,128)(2,1)S(1)}, bf16[2,8,16,768]{3,2,1,0:T(8,128)(2,1)S(1)}, u32[]{:S(2)}, u32[]{:S(2)}) collective-permute-start(bf16[2,8,16,768]{3,2,1,0:T(8,128)(2,1)S(1)} %pad_maximum_fusion.4.refs_1_), channel_id=1, source_target_pairs={{0,3},{1,0},{2,1},{3,2},{4,7},{5,4},{6,5},{7,6},{8,11},{9,8},{10,9... | collective-permute-start | bytes 1179656 | tf_op jit(solution)/shard_map/ppermute | solution.py:32
  38.0 11.2 %collective-permute-start.5 = (bf16[2,8,16,768]{3,2,1,0:T(8,128)(2,1)S(1)}, bf16[2,8,16,768]{3,2,1,0:T(8,128)(2,1)S(1)}, u32[]{:S(2)}, u32[]{:S(2)}) collective-permute-start(bf16[2,8,16,768]{3,2,1,0:T(8,128)(2,1)S(1)} %pad_maximum_fusion.4.refs_1_), channel_id=1, source_target_pairs={{0,1},{1,2},{2,3},{3,0},{4,5},{5,6},{6,7},{7,4},{8,9},{9,10},{10,1... | collective-permute-start | bytes 1179656 | tf_op jit(solution)/shard_map/ppermute | solution.py:32
  38.2 11.0 %collective-permute-start.4 = (bf16[2,8,16,768]{3,2,1,0:T(8,128)(2,1)S(1)}, bf16[2,8,16,768]{3,2,1,0:T(8,128)(2,1)S(1)}, u32[]{:S(2)}, u32[]{:S(2)}) collective-permute-start(bf16[2,8,16,768]{3,2,1,0:T(8,128)(2,1)S(1)} %pad_maximum_fusion.3.refs_0_), channel_id=1, source_target_pairs={{0,3},{1,0},{2,1},{3,2},{4,7},{5,4},{6,5},{7,6},{8,11},{9,8},{10,9... | collective-permute-start | bytes 1179656 | tf_op jit(solution)/shard_map/ppermute | solution.py:32
  75.5 10.2 %collective-permute-start.9 = (bf16[768,384]{1,0:T(8,128)(2,1)S(1)}, bf16[768,384]{1,0:T(8,128)(2,1)S(1)}, u32[]{:S(2)}, u32[]{:S(2)}) collective-permute-start(bf16[768,384]{1,0:T(8,128)(2,1)S(1)} %bitcast.66), channel_id=1, source_target_pairs={{0,4},{1,5},{2,6},{3,7},{4,8},{5,9},{6,10},{7,11},{8,12},{9,13},{1... | collective-permute-start | bytes 1769480 | tf_op jit(solution)/shard_map/ppermute | solution.py:32
  75.6 11.0 %collective-permute-start.11 = (bf16[768,384]{1,0:T(8,128)(2,1)S(1)}, bf16[768,384]{1,0:T(8,128)(2,1)S(1)}, u32[]{:S(2)}, u32[]{:S(2)}) collective-permute-start(bf16[768,384]{1,0:T(8,128)(2,1)S(1)} %bitcast.67), channel_id=1, source_target_pairs={{0,12},{1,13},{2,14},{3,15},{4,0},{5,1},{6,2},{7,3},{8,4},{9,5},{1... | collective-permute-start | bytes 1769480 | tf_op jit(solution)/shard_map/ppermute | solution.py:32
  78.2 16.0 %all-to-all-start.3 = ((bf16[16,16,384]{2,1,0:T(8,128)(2,1)}), bf16[16,16,384]{2,1,0:T(8,128)(2,1)S(1)}, u32[]{:S(2)}, u32[]{:S(2)}) async-start(bf16[16,16,384]{2,1,0:T(8,128)(2,1)} %copy-done.1), calls=%async_computation.3 | async-start | bytes 393216 | tf_op jit(solution)/shard_map/all_to_all | solution.py:483
  85.8 8.4 %collective-permute-start.10 = (bf16[384,384]{1,0:T(8,128)(2,1)S(1)}, bf16[384,384]{1,0:T(8,128)(2,1)S(1)}, u32[]{:S(2)}, u32[]{:S(2)}) collective-permute-start(bf16[384,384]{1,0:T(8,128)(2,1)S(1)} %slice.99), channel_id=1, source_target_pairs={{0,4},{1,5},{2,6},{3,7},{4,8},{5,9},{6,10},{7,11},{8,12},{9,13},{1... | collective-permute-start | bytes 884744 | tf_op jit(solution)/shard_map/ppermute | solution.py:32
  91.3 17.1 %collective-permute-start.13 = (bf16[2,768,384]{2,1,0:T(8,128)(2,1)}, bf16[2,768,384]{2,1,0:T(8,128)(2,1)}, u32[]{:S(2)}, u32[]{:S(2)}) collective-permute-start(bf16[2,768,384]{2,1,0:T(8,128)(2,1)} %pad_maximum_fusion.refs_1_), channel_id=1, source_target_pairs={{0,1},{1,2},{2,3},{3,0},{4,5},{5,6},{6,7},{7,4},{8,9},{9,10},{10,1... | collective-permute-start | bytes 3538952 | tf_op jit(solution)/shard_map/ppermute | solution.py:32
  93.0 16.2 %collective-permute-start.17 = (bf16[2,768,384]{2,1,0:T(8,128)(2,1)}, bf16[2,768,384]{2,1,0:T(8,128)(2,1)}, u32[]{:S(2)}, u32[]{:S(2)}) collective-permute-start(bf16[2,768,384]{2,1,0:T(8,128)(2,1)} %pad_maximum_fusion.refs_1_), channel_id=1, source_target_pairs={{0,3},{1,0},{2,1},{3,2},{4,7},{5,4},{6,5},{7,6},{8,11},{9,8},{10,9... | collective-permute-start | bytes 3538952 | tf_op jit(solution)/shard_map/ppermute | solution.py:32
  95.5 25.5 %collective-permute-start.15 = (bf16[2,768,384]{2,1,0:T(8,128)(2,1)}, bf16[2,768,384]{2,1,0:T(8,128)(2,1)}, u32[]{:S(2)}, u32[]{:S(2)}) collective-permute-start(bf16[2,768,384]{2,1,0:T(8,128)(2,1)} %pad_maximum_fusion.1.refs_2_), channel_id=1, source_target_pairs={{0,1},{1,2},{2,3},{3,0},{4,5},{5,6},{6,7},{7,4},{8,9},{9,10},{10,1... | collective-permute-start | bytes 3538952 | tf_op jit(solution)/shard_map/ppermute | solution.py:32
  96.7 25.1 %collective-permute-start.16 = (bf16[2,768,384]{2,1,0:T(8,128)(2,1)}, bf16[2,768,384]{2,1,0:T(8,128)(2,1)S(1)}, u32[]{:S(2)}, u32[]{:S(2)}) collective-permute-start(bf16[2,768,384]{2,1,0:T(8,128)(2,1)} %pad_maximum_fusion.1.refs_2_), channel_id=1, source_target_pairs={{0,3},{1,0},{2,1},{3,2},{4,7},{5,4},{6,5},{7,6},{8,11},{9,8},{10,9... | collective-permute-start | bytes 3538952 | tf_op jit(solution)/shard_map/ppermute | solution.py:32
  108.4 25.2 %collective-permute-start.14 = (bf16[2,768,384]{2,1,0:T(8,128)(2,1)}, bf16[2,768,384]{2,1,0:T(8,128)(2,1)S(1)}, u32[]{:S(2)}, u32[]{:S(2)}) collective-permute-start(bf16[2,768,384]{2,1,0:T(8,128)(2,1)} %collective-permute-done.13.refs_3_), channel_id=1, source_target_pairs={{0,1},{1,2},{2,3},{3,0},{4,5},{5,6},{6,7},{7,4},{8,9},{9,10},{10,1... | collective-permute-start | bytes 3538952 | tf_op jit(solution)/shard_map/ppermute | solution.py:32
  121.8 16.5 %collective-permute-start.18 = (bf16[2,768,384]{2,1,0:T(8,128)(2,1)S(1)}, bf16[2,768,384]{2,1,0:T(8,128)(2,1)}, u32[]{:S(2)}, u32[]{:S(2)}) collective-permute-start(bf16[2,768,384]{2,1,0:T(8,128)(2,1)S(1)} %collective-permute-done.16.refs_2_), channel_id=1, source_target_pairs={{0,3},{1,0},{2,1},{3,2},{4,7},{5,4},{6,5},{7,6},{8,11},{9,8},{10,9... | collective-permute-start | bytes 3538952 | tf_op jit(solution)/shard_map/ppermute | solution.py:32
  148.8 10.5 %collective-permute-start.19 = (bf16[96,3072]{1,0:T(8,128)(2,1)}, bf16[96,3072]{1,0:T(8,128)(2,1)S(1)}, u32[]{:S(2)}, u32[]{:S(2)}) collective-permute-start(bf16[96,3072]{1,0:T(8,128)(2,1)} %get-tuple-element.61), channel_id=1, source_target_pairs={{0,4},{1,5},{2,6},{3,7},{4,8},{5,9},{6,10},{7,11},{8,12},{9,13},{1... | collective-permute-start | bytes 1769480 | tf_op jit(solution)/shard_map/ppermute | solution.py:32
  148.9 10.4 %collective-permute-start.20 = (bf16[96,3072]{1,0:T(8,128)(2,1)}, bf16[96,3072]{1,0:T(8,128)(2,1)S(1)}, u32[]{:S(2)}, u32[]{:S(2)}) collective-permute-start(bf16[96,3072]{1,0:T(8,128)(2,1)} %get-tuple-element.62), channel_id=1, source_target_pairs={{0,12},{1,13},{2,14},{3,15},{4,0},{5,1},{6,2},{7,3},{8,4},{9,5},{1... | collective-permute-start | bytes 1769480 | tf_op jit(solution)/shard_map/ppermute | solution.py:32
  159.3 10.5 %collective-permute-start.23 = (bf16[96,3072]{1,0:T(8,128)(2,1)}, bf16[96,3072]{1,0:T(8,128)(2,1)S(1)}, u32[]{:S(2)}, u32[]{:S(2)}) collective-permute-start(bf16[96,3072]{1,0:T(8,128)(2,1)} %get-tuple-element.68), channel_id=1, source_target_pairs={{0,4},{1,5},{2,6},{3,7},{4,8},{5,9},{6,10},{7,11},{8,12},{9,13},{1... | collective-permute-start | bytes 1769480 | tf_op jit(solution)/shard_map/ppermute | solution.py:32
  159.3 10.9 %collective-permute-start.25 = (bf16[96,3072]{1,0:T(8,128)(2,1)}, bf16[96,3072]{1,0:T(8,128)(2,1)S(1)}, u32[]{:S(2)}, u32[]{:S(2)}) collective-permute-start(bf16[96,3072]{1,0:T(8,128)(2,1)} %get-tuple-element.70), channel_id=1, source_target_pairs={{0,12},{1,13},{2,14},{3,15},{4,0},{5,1},{6,2},{7,3},{8,4},{9,5},{1... | collective-permute-start | bytes 1769480 | tf_op jit(solution)/shard_map/ppermute | solution.py:32
  162.3 20.1 %collective-permute-start.21 = (bf16[192,3072]{1,0:T(8,128)(2,1)S(1)}, bf16[192,3072]{1,0:T(8,128)(2,1)S(1)}, u32[]{:S(2)}, u32[]{:S(2)}) collective-permute-start(bf16[192,3072]{1,0:T(8,128)(2,1)S(1)} %fusion.5), channel_id=1, source_target_pairs={{0,4},{1,5},{2,6},{3,7},{4,8},{5,9},{6,10},{7,11},{8,12},{9,13},{1... | collective-permute-start | bytes 3538952 | tf_op jit(solution)/shard_map/ppermute | solution.py:32
  162.8 19.7 %collective-permute-start.22 = (bf16[192,3072]{1,0:T(8,128)(2,1)S(1)}, bf16[192,3072]{1,0:T(8,128)(2,1)S(1)}, u32[]{:S(2)}, u32[]{:S(2)}) collective-permute-start(bf16[192,3072]{1,0:T(8,128)(2,1)S(1)} %fusion.6), channel_id=1, source_target_pairs={{0,12},{1,13},{2,14},{3,15},{4,0},{5,1},{6,2},{7,3},{8,4},{9,5},{1... | collective-permute-start | bytes 3538952 | tf_op jit(solution)/shard_map/ppermute | solution.py:32
  170.1 24.9 %collective-permute-start.24 = (bf16[192,3072]{1,0:T(8,128)(2,1)S(1)}, bf16[192,3072]{1,0:T(8,128)(2,1)S(1)}, u32[]{:S(2)}, u32[]{:S(2)}) collective-permute-start(bf16[192,3072]{1,0:T(8,128)(2,1)S(1)} %fusion.7), channel_id=1, source_target_pairs={{0,4},{1,5},{2,6},{3,7},{4,8},{5,9},{6,10},{7,11},{8,12},{9,13},{1... | collective-permute-start | bytes 3538952 | tf_op jit(solution)/shard_map/ppermute | solution.py:32
  170.5 24.5 %collective-permute-start.26 = (bf16[192,3072]{1,0:T(8,128)(2,1)S(1)}, bf16[192,3072]{1,0:T(8,128)(2,1)S(1)}, u32[]{:S(2)}, u32[]{:S(2)}) collective-permute-start(bf16[192,3072]{1,0:T(8,128)(2,1)S(1)} %fusion.8), channel_id=1, source_target_pairs={{0,12},{1,13},{2,14},{3,15},{4,0},{5,1},{6,2},{7,3},{8,4},{9,5},{1... | collective-permute-start | bytes 3538952 | tf_op jit(solution)/shard_map/ppermute | solution.py:32
  196.9 10.9 %collective-permute-start.27 = (bf16[48,6144]{1,0:T(8,128)(2,1)}, bf16[48,6144]{1,0:T(8,128)(2,1)}, u32[]{:S(2)}, u32[]{:S(2)}) collective-permute-start(bf16[48,6144]{1,0:T(8,128)(2,1)} %get-tuple-element.79), channel_id=1, source_target_pairs={{0,2},{1,3},{2,0},{3,1},{4,6},{5,7},{6,4},{7,5},{8,10},{9,11},{10,... | collective-permute-start | bytes 1769480 | tf_op jit(solution)/shard_map/ppermute | solution.py:32
  198.0 16.0 %collective-permute-start.28 = (bf16[48,6144]{1,0:T(8,128)(2,1)}, bf16[48,6144]{1,0:T(8,128)(2,1)}, u32[]{:S(2)}, u32[]{:S(2)}) collective-permute-start(bf16[48,6144]{1,0:T(8,128)(2,1)} %get-tuple-element.81), channel_id=1, source_target_pairs={{0,1},{1,2},{2,3},{3,0},{4,5},{5,6},{6,7},{7,4},{8,9},{9,10},{10,1... | collective-permute-start | bytes 1769480 | tf_op jit(solution)/shard_map/ppermute | solution.py:32
  200.7 14.2 %collective-permute-start.29 = (bf16[48,6144]{1,0:T(8,128)(2,1)S(1)}, bf16[48,6144]{1,0:T(8,128)(2,1)}, u32[]{:S(2)}, u32[]{:S(2)}) collective-permute-start(bf16[48,6144]{1,0:T(8,128)(2,1)S(1)} %get-tuple-element.80), channel_id=1, source_target_pairs={{0,3},{1,0},{2,1},{3,2},{4,7},{5,4},{6,5},{7,6},{8,11},{9,8},{10,9... | collective-permute-start | bytes 1769480 | tf_op jit(solution)/shard_map/ppermute | solution.py:32
  217.8 21.4 %all-to-all-start.4 = ((bf16[8,6,6144]{2,1,0:T(8,128)(2,1)}), bf16[8,6,6144]{2,1,0:T(8,128)(2,1)S(1)}, u32[]{:S(2)}, u32[]{:S(2)}) async-start(bf16[8,6,6144]{2,1,0:T(8,128)(2,1)} %reshape.174), calls=%async_computation.4 | async-start | bytes 1572864 | tf_op jit(solution)/shard_map/all_to_all | solution.py:527
  (23 other events, 208.8 us)
Sparse Core Ops, SparseCore 0:
  9.0 37.8 all-gather.2
